TPU v7x, 32 devices: a whole 2x2x4 slice. The times are simulated.
32 devices in a mesh: band: 4 (over x, core), grid: 8 (over z, y).
Axes of the slice: x: 2, y: 2, z: 4, core: 2. Of those that a mesh axis runs over, the one named last changes fastest.
Arguments:
- orbitals: float32 [96, 16, 16, 512], P('grid', None, None, 'band'), may hold values from -24 to 24
- potential: float32 [96, 16, 16], P('grid'), may hold values from -3 to -1
- projectors: float32 [32, 8, 13, 256], P('grid'), may hold values from -0.109375 to 0.109375
- atom_planes: int32 [32, 13], P('grid'), may hold values from 0 to 23, as said below
- kb_energy: float32 [8], replicated, may hold values from 1 to 4
Outputs:
- filtered: float32 [96, 16, 16, 512], P('grid', None, None, 'band')
- correlation_gram: float32 [512, 512], P('band')
Inputs may be any that keep to these rules, and one draw needn't show every extreme that they name: `atom_planes`: each atom's row holds 13 consecutive plane numbers; the first atom starts at plane 0 and the last atom at plane 12 - 1.
All inputs are finite; a program needn't handle non-finite values.
Results may differ from a plain program's by a relative error of at most 0.0003.
Values sent between devices are 32-bit elements; how exact they have to be, the bound alone decides.
No kernel may reach another device: no remote copies, remote signals or barrier semaphores. Data moves between devices by JAX's collectives and lax.ppermute only.
A program may use at most 128 MiB of HBM per device.

v0:
```python
import functools

import jax
import jax.numpy as jnp
import ml_dtypes
import numpy as np
from jax import lax
from jax.experimental import pallas as pl
from jax.experimental.pallas import tpu as pltpu
from jax.sharding import PartitionSpec as P

DEGREE = 4
REACH = 6
LANES = 128
QUARTER = 32

WEIGHTS = (
    -5369.0 / 1800.0,
    12.0 / 7.0,
    -15.0 / 56.0,
    10.0 / 189.0,
    -1.0 / 112.0,
    2.0 / 1925.0,
    -1.0 / 16632.0,
)
LOWER = -4.0
CUTOFF = 1.0
UPPER = 16.0
F32 = jnp.float32
BF16 = jnp.bfloat16


def filter_terms(degree):
    half_span = (UPPER - CUTOFF) / 2.0
    middle = (UPPER + CUTOFF) / 2.0
    sigma_now = half_span / (LOWER - middle)
    sigma_first = sigma_now
    scales = [sigma_now / half_span]
    recall = [0.0]
    for level in range(1, degree):
        sigma_next = 1.0 / (2.0 / sigma_first - sigma_now)
        scales.append(2.0 * sigma_next / half_span)
        recall.append(sigma_now * sigma_next)
        sigma_now = sigma_next
    return (middle, scales, recall)


def plane_matrix(ny, nz):
    def ring(n):
        m = np.zeros((n, n))
        for i in range(n):
            m[i, i] += WEIGHTS[0]
            for r in range(1, REACH + 1):
                m[i, (i + r) % n] += WEIGHTS[r]
                m[i, (i - r) % n] += WEIGHTS[r]
        return m

    full = -0.5 * (np.kron(ring(ny), np.eye(nz)) + np.kron(np.eye(ny), ring(nz)))
    high = full.astype(ml_dtypes.bfloat16)
    low = (full - high.astype(np.float64)).astype(ml_dtypes.bfloat16)
    return high, low


def halves(value):
    high = value.astype(BF16)
    return high, (value - high.astype(F32)).astype(BF16)


def dot3(*pairs):
    left, right = [], []
    for (a_high, a_low), (b_high, b_low) in pairs:
        left += [a_high, a_high, a_low]
        right += [b_high, b_low, b_high]
    return lax.dot_general(
        jnp.concatenate(left, axis=1),
        jnp.concatenate(right, axis=0),
        (((1,), (0,)), ((), ())),
        preferred_element_type=F32,
    )


def lane_ids(shape):
    return lax.broadcasted_iota(jnp.int32, shape, len(shape) - 1)


def turn(value, shift):
    if isinstance(shift, int):
        shift = shift % LANES
        if shift == 0:
            return value
    else:
        shift = lax.rem(shift + 8 * LANES, LANES)
    return pltpu.roll(value, shift, axis=value.ndim - 1)


def pack_kernel(chunk, y_ref, x_ref, *refs):
    y = y_ref[0]
    out_ref = refs[-1]
    cells = x_ref.shape[1]
    group = lane_ids((cells, LANES)) // QUARTER
    if len(refs) > 1:
        out_ref[3 * cells :] = refs[0][...]
    for r in range(3):
        row = None
        for slot, plane in enumerate((r, r + 6, r + 3, r + 9)):
            piece = turn(x_ref[plane], QUARTER * slot - 64 - QUARTER * chunk + 64 * y)
            row = piece if row is None else jnp.where(group == slot, piece, row)
        out_ref[r * cells : (r + 1) * cells] = row


def rim_pack(row, out_ref, r, source):
    part = row.shape[0] // 4
    group = lane_ids((part, LANES)) // QUARTER
    packed = None
    for j in range(4):
        piece = turn(row[j * part : (j + 1) * part], QUARTER * (j - source))
        packed = piece if packed is None else jnp.where(group == j, piece, packed)
    out_ref[pl.ds(r * part, part), :] = packed


def assemble_kernel(chunk, y_ref, x_ref, got_ref, *refs):
    y = y_ref[0]
    mh_ref, ml_ref, v_ref, up_ref, down_ref, coef_ref = refs
    cells = x_ref.shape[1]
    group = lane_ids((cells, LANES)) // QUARTER
    coef = None
    for r in range(6):
        first = turn(x_ref[r], -QUARTER * chunk)
        second = turn(x_ref[r + 6], QUARTER - QUARTER * chunk)
        other = turn(
            got_ref[cells * (r % 3) : cells * (r % 3 + 1)], 64 * (1 - y) if r < 3 else 64 * y
        )
        row = jnp.where(group == 2 * y, first, jnp.where(group == 2 * y + 1, second, other))
        v_ref[r] = row
        rim_pack(row, up_ref, r, 3)
        rim_pack(row, down_ref, r, 0)
        term = dot3(((mh_ref[r], ml_ref[r]), halves(row)))
        coef = term if coef is None else coef + term
    share_coef(coef, coef_ref, up_ref, down_ref)


def share_coef(coef, coef_ref, up_ref, down_ref):
    packed = collapse(coef)
    coef_ref[...] = packed
    rim = up_ref.shape[0] - 16
    group = lane_ids((16, LANES)) // QUARTER
    top, bottom = packed[:16], packed[16:]
    up_ref[pl.ds(rim, 16), :] = jnp.where(group % 2 == 0, turn(top, -QUARTER), bottom)
    down_ref[pl.ds(rim, 16), :] = jnp.where(group % 2 == 0, top, turn(bottom, QUARTER))


def collapse(blocks):
    group = lane_ids((32, LANES)) // QUARTER

    def block(i, s, target):
        b = 2 * i + s
        return turn(blocks[32 * b : 32 * b + 32], QUARTER * (target - i))

    low = block(0, 0, 0) + block(1, 0, 0) + block(2, 0, 0)
    high = block(1, 1, 1) + block(2, 1, 1) + block(3, 1, 1)
    below, above = block(0, 1, 2), block(3, 0, 3)
    return jnp.where(
        group == 0, low, jnp.where(group == 1, high, jnp.where(group == 2, below, above))
    )


def level_kernel(scale, recall, first, last, *refs):
    refs = list(refs)
    if last:
        yx_ref = refs.pop(0)
    v_ref = refs.pop(0)
    prev_ref = None if first else refs.pop(0)
    below_ref, above_ref = refs.pop(0), refs.pop(0)
    own_ref, kb_ref, ch_ref, cl_ref, th_ref, tl_ref, pot_ref = refs[:7]
    refs = refs[7:]
    if last:
        own_piece, y_piece, x_piece, d_piece, ext = refs
    else:
        mh_ref, ml_ref, out_ref, up_ref, down_ref, coef_ref, ext = refs
    cells = v_ref.shape[1]
    part = cells // 4
    rim = 6 * part
    part_group = lane_ids((part, LANES)) // QUARTER
    cg = lane_ids((32, LANES)) // QUARTER
    low, high = below_ref[pl.ds(rim, 16), :], above_ref[pl.ds(rim, 16), :]
    from_below = jnp.concatenate([turn(low, 2 * QUARTER), turn(low, QUARTER)], axis=0)
    from_above = jnp.concatenate([turn(high, -QUARTER), turn(high, 2 * QUARTER)], axis=0)
    total = own_ref[...] + jnp.where(cg % 2 == 0, from_below, from_above)
    total = total * kb_ref[...]
    rows = []
    for i, s, source in (
        (0, 0, 0), (0, 1, 2), (1, 0, 0), (1, 1, 1), (2, 0, 0), (2, 1, 1), (3, 0, 3), (3, 1, 1),
    ):
        rows.append(jnp.where(cg == i, turn(total, QUARTER * (i - source)), 0.0))
    spread = halves(jnp.concatenate(rows, axis=0))
    for r in range(6):
        row = v_ref[r]
        ext[6 + r] = row
        before, after = turn(row, QUARTER), turn(row, -QUARTER)
        low, high = below_ref[pl.ds(r * part, part), :], above_ref[pl.ds(r * part, part), :]
        for j in range(4):
            cut = slice(j * part, (j + 1) * part)
            ext[r, cut] = jnp.where(part_group == 0, turn(low, -QUARTER * j), before[cut])
            ext[12 + r, cut] = jnp.where(part_group == 3, turn(high, 96 - QUARTER * j), after[cut])
    coef = None
    pot = pot_ref[...]
    if last:
        mine = 2 * yx_ref[0] + yx_ref[1]
    for r in range(6):
        row = ext[6 + r]
        value = dot3(
            ((ch_ref[...], cl_ref[...]), halves(row)), ((th_ref[r], tl_ref[r]), spread)
        )
        value = value + potential_row(pot, r) * row
        for k in range(1, REACH + 1):
            value = value + (-0.5 * WEIGHTS[k]) * (ext[6 + r + k] + ext[6 + r - k])
        value = scale * value
        if not first:
            value = value - recall * prev_ref[r]
        if last:
            for flip, piece in enumerate((own_piece, x_piece, y_piece, d_piece)):
                rim_pack(value, piece, r, lax.bitwise_xor(mine, flip))
        else:
            out_ref[r] = value
            rim_pack(value, up_ref, r, 3)
            rim_pack(value, down_ref, r, 0)
            term = dot3(((mh_ref[r], ml_ref[r]), halves(value)))
            coef = term if coef is None else coef + term
    if not last:
        share_coef(coef, coef_ref, up_ref, down_ref)


def unpack_kernel(
    yx_ref, own0_ref, own1_ref, x0_ref, x1_ref, y0_ref, y1_ref, rest_ref, out_ref
):
    y, x = yx_ref[0], yx_ref[1]
    cells = out_ref.shape[1]
    part = cells // 4
    rim = 6 * part
    group = lane_ids((part, LANES)) // QUARTER
    rest = [rest_ref.at[pl.ds(k * rim, rim)] for k in range(2)]
    for half, own, got in (
        (x, (own0_ref, own1_ref), (y0_ref, y1_ref)),
        (1 - x, (x0_ref, x1_ref), rest),
    ):
        for r in range(6):
            for j in range(4):
                block = None
                for k in range(2):
                    here = turn(own[k][pl.ds(r * part, part), :], 64 * y + QUARTER * (k - j))
                    there = turn(got[k][pl.ds(r * part, part), :], 64 * (1 - y) + QUARTER * (k - j))
                    mine = jnp.where(group == 2 * y + k, here, there)
                    block = mine if k == 0 else jnp.where(group % 2 == 1, mine, block)
                out_ref[6 * half + r, j * part : (j + 1) * part] = block


def tile_kernel(y_ref, own_ref, x_ref, y_piece_ref, d_ref, *refs):
    y = y_ref[0]
    rows = own_ref.shape[0]
    out_ref = refs[2] if len(refs) > 2 else refs[0]
    if len(refs) > 2:
        refs[3][:rows] = refs[0][...]
        refs[3][rows:] = refs[1][...]
    pieces = [own_ref[...], y_piece_ref[...], x_ref[...], d_ref[...]]
    group = lane_ids((rows, LANES)) // QUARTER
    for j in range(4):
        block = None
        for s, piece in enumerate(pieces):
            target = 2 * (s // 2) + lax.bitwise_xor(y, s % 2)
            turned = turn(piece, QUARTER * (target - j))
            block = turned if block is None else jnp.where(group == target, turned, block)
        out_ref[pl.ds(j * rows, rows), :] = block


def gram_product(left, right):
    def dot(p, q):
        return lax.dot_general(p, q, (((0,), (0,)), ((), ())), preferred_element_type=F32)

    def side(parts, i):
        return jnp.concatenate([p[i] for p in parts], axis=1)

    high, low = side(left, 0), side(left, 1)
    return dot(high, side(right, 0)) + (dot(high, side(right, 1)) + dot(low, side(right, 0)))


def gram_early_kernel(a0_ref, a1_ref, s0_ref, out_ref):
    parts = [halves(ref[...]) for ref in (a0_ref, a1_ref, s0_ref)]
    out_ref[...] = gram_product(parts[:2], parts)


def gram_kernel(
    y_ref, a0_ref, a1_ref, s1_ref, early_ref, own_ref, to_y_ref, to_x_ref, to_d_ref, parts_ref
):
    parts = [halves(ref[...]) for ref in (a0_ref, a1_ref, s1_ref)]
    late = gram_product(parts[:2], parts[2:])
    total = jnp.concatenate([early_ref[...], late], axis=1)
    group = lane_ids((32, LANES)) // QUARTER
    for x_row in range(2):
        for h_row in range(2):
            for k_row in range(2):
                at = 128 * k_row + 64 * x_row + 32 * h_row
                for flip in range(4):
                    x_col, core = flip // 2, flip % 2
                    block = None
                    for h in range(2):
                        for k in range(2):
                            start = 256 * core + 128 * k
                            tile = total[at : at + 32, start : start + 128]
                            piece = turn(tile, QUARTER * (2 * h + k - 2 * x_col - h))
                            block = (
                                piece
                                if block is None
                                else jnp.where(group == 2 * h + k, piece, block)
                            )
                    to = 2 * (x_col ^ x_row) + core
                    rows = slice(32 * k_row, 32 * k_row + 32)
                    parts_ref[2 * x_row + h_row, rows, 128 * to : 128 * to + 128] = block
    y = y_ref[0]
    own_ref[...] = parts_ref[y]
    to_y_ref[...] = parts_ref[1 - y]
    to_x_ref[...] = parts_ref[2 + y]
    to_d_ref[...] = parts_ref[3 - y]


def add_kernel(*refs):
    *terms, out_ref = refs
    out_ref[...] = (terms[0][...] + terms[1][...]) + (terms[2][...] + terms[3][...])


def ring_add_kernel(factor, z_ref, *refs):
    *terms, out_ref, slots = refs
    count = len(terms)
    for k, term in enumerate(terms):
        slots[lax.rem(z_ref[0] - k + count, count)] = term[...]
    total = slots[0]
    for k in range(1, count):
        total = total + slots[k]
    out_ref[...] = total * factor


def scale_kernel(factor, in_ref, out_ref):
    out_ref[...] = in_ref[...] * factor


def order_kernel(yb_ref, mine_ref, got_ref, out_ref):
    y, b = yb_ref[0], yb_ref[1]
    half = mine_ref.shape[0]
    for ref, h in ((mine_ref, y), (got_ref, 1 - y)):
        rows = pl.ds(pl.multiple_of(half * h, half), half)
        for j in range(4):
            to = pl.multiple_of(lax.bitwise_xor(b, j) * 128, 128)
            out_ref[rows, pl.ds(to, 128)] = ref[:, j * 128 : (j + 1) * 128]


def dense_kernel(yc_ref, planes_ref, proj_ref, pot_ref, e_ref, part_ref, rim_ref):
    y, c = yc_ref[0], yc_ref[1]
    e_ref[...] = jnp.zeros_like(e_ref)
    atoms, span, count, _ = proj_ref.shape
    for a in range(atoms):
        for b in range(span):
            at = (planes_ref[a, b], slice(a * count, (a + 1) * count))
            e_ref[at] = e_ref[at] + proj_ref[a, b]
    rows = pl.ds(pl.multiple_of(16 * c, 16), 16)
    for r in range(18):
        part_ref[r] = e_ref[6 * (1 - y) + r, rows, :]
    part_ref[18] = jnp.zeros(part_ref.shape[1:], F32)
    part_ref[18, : pot_ref.shape[0]] = pot_ref[...]
    rim_ref[...] = e_ref[pl.ds(18 * y, 6), rows, :]


def potential_kernel(offset, y_ref, own_ref, part_ref, out_ref):
    y = y_ref[0]
    own = own_ref[...] + offset
    other = part_ref[18, : own.shape[0]] + offset
    first, second = jnp.where(y == 0, own, other), jnp.where(y == 0, other, own)
    fill = jnp.zeros((8, own.shape[1]), F32)
    planes = jnp.concatenate([first, second, fill], axis=0)
    parts = []
    for _ in range(3):
        piece = planes.astype(BF16).astype(F32)
        parts.append(piece)
        planes = planes - piece
    out_ref[...] = jnp.concatenate(parts + [jnp.zeros_like(planes)], axis=0).T.astype(BF16)


def potential_row(pot, r):
    source = lax.broadcasted_iota(jnp.int32, (LANES, LANES), 0)
    group = lane_ids((LANES, LANES)) // QUARTER
    pick = (source % QUARTER == 6 * group + r) & (source < 3 * QUARTER)
    return lax.dot_general(
        pot, pick.astype(F32).astype(BF16), (((1,), (0,)), ((), ())), preferred_element_type=F32
    )


def gather_kernel(y_ref, part_ref, a_ref, b_ref, out_ref):
    y = y_ref[0]
    out_ref[:18] = part_ref[:18]
    for r in range(6):
        one, two = a_ref[r], b_ref[r]
        out_ref[18 + r] = jnp.where(y == 1, one, two)
        out_ref[24 + r] = jnp.where(y == 1, two, one)


def maps_kernel(yc_ref, e_ref, part_ref, part2_ref, mh_ref, ml_ref, th_ref, tl_ref):
    y, c = yc_ref[0], yc_ref[1]

    def whole(plane):
        mine, rest = part_ref[plane], part2_ref[plane]
        first, second = jnp.where(c == 0, mine, rest), jnp.where(c == 0, rest, mine)
        return jnp.concatenate([first, second], axis=0)

    for r in range(6):
        below, above = whole(18 + r), whole(24 + r)
        other = [whole(6 * i + r) for i in range(3)]
        low = [jnp.where(y == 0, e_ref[6 + 6 * i + r], other[i]) for i in range(3)]
        high = [jnp.where(y == 1, e_ref[6 * i + r], other[i]) for i in range(3)]
        block = jnp.concatenate(
            [low[0], below, low[1], high[0], low[2], high[1], above, high[2]], axis=0
        )
        mh_ref[r], ml_ref[r] = halves(block)
        th_ref[r], tl_ref[r] = halves(block.T)


SMEM = pl.BlockSpec(memory_space=pltpu.SMEM)
VMEM = pl.BlockSpec(memory_space=pltpu.VMEM)
ANY = pl.BlockSpec(memory_space=pl.ANY)


def call(kernel, out, scalars, arrays, scratch=(), after=()):
    used = len(scalars) + len(arrays)

    def body(*refs):
        kernel(*refs[:used], *refs[used + len(after) :])

    return pl.pallas_call(
        body,
        out_shape=out,
        in_specs=[SMEM] * len(scalars) + [VMEM] * len(arrays) + [ANY] * len(after),
        out_specs=[VMEM] * len(out),
        scratch_shapes=list(scratch),
        compiler_params=pltpu.CompilerParams(vmem_limit_bytes=16 * 1024 * 1024),
        cost_estimate=pl.CostEstimate(flops=1 << 10, bytes_accessed=1 << 10, transcendentals=0),
    )(*scalars, *arrays, *after)


def f32(*shape):
    return pltpu.VMEM(shape, F32)


def bf16(*shape):
    return pltpu.VMEM(shape, BF16)


def shards(orbitals, potential, projectors, atom_planes, kb_energy):
    slab, ny, nz, orb_here = orbitals.shape
    cells = ny * nz
    peers = lax.axis_size("grid")
    bands = lax.axis_size("band")
    g, b = lax.axis_index("grid"), lax.axis_index("band")
    y, c, x = lax.rem(g, 2), lax.rem(b, 2), b // 2
    y1 = y.reshape(1).astype(jnp.int32)
    z1 = (g // 2).reshape(1).astype(jnp.int32)
    yb = jnp.stack([y, b]).astype(jnp.int32)
    yc = jnp.stack([y, c]).astype(jnp.int32)
    yx = jnp.stack([y, x]).astype(jnp.int32)

    def move(array, axis, target):
        size = lax.axis_size(axis)
        return lax.ppermute(array, axis, [(i, target(i) % size) for i in range(size)])

    def partner(array):
        return move(array, "grid", lambda i: i ^ 1)

    def up(array):
        return move(array, "grid", lambda i: i + 2)

    def down(array):
        return move(array, "grid", lambda i: i - 2)

    def sibling(array):
        return move(array, "band", lambda i: i ^ 1)

    def across(array):
        return move(array, "band", lambda i: i ^ 2)

    field = orbitals.reshape(slab, cells, orb_here)
    rim_rows = 6 * (cells // 4)
    middle, scales, recall = filter_terms(DEGREE)

    def diagonal(array):
        size = peers * bands
        flip = 2 * peers + 1
        return lax.ppermute(array, ("band", "grid"), [(i, i ^ flip) for i in range(size)])

    pot_own = potential.reshape(slab, cells)
    sent0 = call(
        functools.partial(pack_kernel, 0), [f32(3 * cells, LANES)], [y1], [field]
    )[0]
    other0 = partner(sent0)
    dense, part, rim = call(
        dense_kernel,
        [f32(24, 32, cells), f32(19, 16, cells), f32(6, 16, cells)],
        [yc, atom_planes],
        [projectors.transpose(0, 2, 1, 3), pot_own],
        after=[sent0],
    )
    part = partner(part)
    rim_a = move(rim, "grid", lambda i: i + 2 if i % 2 else i - 2)
    rim_b = move(rim, "grid", lambda i: i + 1 if i % 2 else i - 1)
    sent1 = call(
        functools.partial(pack_kernel, 1),
        [f32(3 * cells, LANES)],
        [y1],
        [field],
        after=[other0],
    )[0]
    other1 = partner(sent1)
    pot_part = part
    part = call(
        gather_kernel, [f32(30, 16, cells)], [y1], [part, rim_a, rim_b], after=[sent1]
    )[0]
    mh, ml, th, tl = call(
        maps_kernel,
        [bf16(6, 256, cells)] * 2 + [bf16(6, cells, 256)] * 2,
        [yc],
        [dense, part, sibling(part)],
    )
    pot = call(
        functools.partial(potential_kernel, -(middle + 0.5 * WEIGHTS[0])),
        [bf16(cells, LANES)],
        [y1],
        [pot_own, pot_part],
        after=[mh],
    )[0]
    kb = jnp.broadcast_to(jnp.tile(kb_energy, 4)[:, None], (32, LANES))
    ch, cl = (jnp.asarray(m) for m in plane_matrix(ny, nz))

    chunks = []
    for k, got in enumerate((other0, other1)):
        made = call(
            functools.partial(assemble_kernel, k),
            [f32(6, cells, LANES)] + [f32(rim_rows + 16, LANES)] * 2 + [f32(32, LANES)],
            [y1],
            [field, got, mh, ml],
            after=[pot] if k else [],
        )
        chunks.append(
            dict(v=made[0], prev=None, below=up(made[1]), above=down(made[2]), coef=made[3])
        )

    for level in range(DEGREE):
        first, last = level == 0, level == DEGREE - 1
        for s in chunks:
            arrays = [s["v"]] + ([] if first else [s["prev"]]) + [s["below"], s["above"]]
            arrays += [s["coef"], kb, ch, cl, th, tl, pot]
            if last:
                out = [f32(rim_rows, LANES)] * 4
            else:
                arrays += [mh, ml]
                out = [f32(6, cells, LANES)] + [f32(rim_rows + 16, LANES)] * 2 + [f32(32, LANES)]
            made = call(
                functools.partial(level_kernel, scales[level], recall[level], first, last),
                out,
                [yx] if last else [],
                arrays,
                [pltpu.VMEM((18, cells, LANES), F32)],
            )
            if last:
                own, for_y, for_x, rest = made
                s["pieces"] = [own, across(for_x), partner(for_y), diagonal(rest)]
                s["for_x"], s["rest"] = for_x, rest
            else:
                s["prev"], s["v"] = s["v"], made[0]
                s["coef"], s["below"], s["above"] = made[3], up(made[1]), down(made[2])

    tile0, rest = call(
        tile_kernel,
        [f32(4 * rim_rows, LANES), f32(2 * rim_rows, LANES)],
        [y1],
        chunks[0]["pieces"] + [s["rest"] for s in chunks],
    )
    tile1 = call(tile_kernel, [f32(4 * rim_rows, LANES)], [y1], chunks[1]["pieces"])[0]
    early = call(
        gram_early_kernel, [f32(256, 384)], [], [tile0, tile1, sibling(tile0)]
    )[0]
    quarters = call(
        gram_kernel,
        [f32(64, bands * 128)] * 4,
        [y1],
        [tile0, tile1, sibling(tile1), early],
        [pltpu.VMEM((4, 64, bands * 128), F32)],
    )
    partial = call(
        add_kernel,
        [f32(64, bands * 128)],
        [],
        [quarters[0], partner(quarters[1]), across(quarters[2]), diagonal(quarters[3])],
    )[0]
    rest, partial = lax.optimization_barrier((rest, partial))
    rest = partner(rest)
    factor = 1.0 / (slab * cells * peers)
    pairs = peers // 2
    if pairs <= 4:
        moved = [partial]
        for k in range(1, pairs):
            moved.append(move(partial, "grid", lambda i, k=k: i + 2 * k))
        total = call(
            functools.partial(ring_add_kernel, factor),
            [f32(64, bands * 128)],
            [z1],
            moved,
            [pltpu.VMEM((pairs, 64, bands * 128), F32)],
            after=[rest],
        )[0]
    else:
        groups = [[2 * i + j for i in range(pairs)] for j in range(2)]
        total = lax.psum(partial, "grid", axis_index_groups=groups)
        total = call(
            functools.partial(scale_kernel, factor), [f32(64, bands * 128)], [], [total]
        )[0]
    gram = call(
        order_kernel,
        [jax.ShapeDtypeStruct((128, bands * 128), F32)],
        [yb],
        [total, partner(total)],
    )[0]
    filtered = call(
        unpack_kernel,
        [jax.ShapeDtypeStruct((slab, cells, LANES), F32)],
        [yx],
        [s["pieces"][0] for s in chunks]
        + [s["for_x"] for s in chunks]
        + [s["pieces"][2] for s in chunks]
        + [rest],
    )[0]
    return (filtered.reshape(orbitals.shape), gram)


def solution(mesh):
    return jax.shard_map(
        shards,
        mesh=mesh,
        in_specs=(
            P("grid", None, None, "band"),
            P("grid", None, None),
            P("grid", None, None, None),
            P("grid", None),
            P(),
        ),
        out_specs=(P("grid", None, None, "band"), P("band", None)),
        check_vma=False,
    )
```

profile of v0, /device:TPU:0, one launch (start us, length us, event | category | flops | bytes accessed | tf_op | source)
XLA Modules:
  0.0 154.6 jit_solution(1287880534524184717)
XLA Ops:
  2.5 3.0 %collective-permute-start = (f32[768,128]{1,0:T(8,128)S(1)}, f32[768,128]{1,0:T(8,128)S(1)}, u32[]{:S(2)}, u32[]{:S(2)}) collective-permute-start(f32[768,128]{1,0:T(8,128)S(1)} %shard_map.86.refs_4_), channel_id=1, source_target_pairs={{0,1},{1,0},{2,3},{3,2},{4,5},{5,4},{6,7},{7,6},{8,9},{9,8},{10,11... | collective-permute-start | bytes 1179656 | tf_op jit(solution)/shard_map/ppermute | solution.py:469
  7.6 4.1 %collective-permute-start.2 = (f32[6,16,256]{2,1,0:T(8,128)S(1)}, f32[6,16,256]{2,1,0:T(8,128)S(1)}, u32[]{:S(2)}, u32[]{:S(2)}) collective-permute-start(f32[6,16,256]{2,1,0:T(8,128)S(1)} %get-tuple-element.59), channel_id=1, source_target_pairs={{0,6},{1,3},{2,0},{3,5},{4,2},{5,7},{6,4},{7,1},{8,14},{9,11},{10,... | collective-permute-start | bytes 294920 | tf_op jit(solution)/shard_map/ppermute | solution.py:469
  12.9 4.4 %collective-permute-done.refs_2_ = f32[768,128]{1,0:T(8,128)S(1)} collective-permute-done((f32[768,128]{1,0:T(8,128)S(1)}, f32[768,128]{1,0:T(8,128)S(1)}, u32[]{:S(2)}, u32[]{:S(2)}) %collective-permute-start) | collective-permute-done | bytes 393248 | tf_op jit(solution)/shard_map/ppermute | solution.py:469
  19.1 4.4 %collective-permute-done.1.refs_1_.refs_2_ = f32[19,16,256]{2,1,0:T(8,128)S(1)} collective-permute-done((f32[19,16,256]{2,1,0:T(8,128)S(1)}, f32[19,16,256]{2,1,0:T(8,128)S(1)}, u32[]{:S(2)}, u32[]{:S(2)}) %collective-permute-start.1) | collective-permute-done | bytes 311328 | tf_op jit(solution)/shard_map/ppermute | solution.py:469
  26.5 1.9 %shard_map.91 = (f32[6,256,128]{2,1,0:T(8,128)S(1)}, f32[400,128]{1,0:T(8,128)}, f32[400,128]{1,0:T(8,128)}, f32[32,128]{1,0:T(8,128)S(1)}) custom-call(s32[1]{0:T(128)} %bitcast.refs_0_, f32[12,256,128]{2,1,0:T(8,128)S(1)} %bitcast.10, f32[768,128]{1,0:T(8,128)S(1)} %collective-permute-done.refs_2_, ...), custom_call_target="tpu_custom_call" | custom-call | flops 1024 | bytes 1024 | tf_op jit(solution)/shard_map/pallas_call | solution.py:435
  31.1 2.0 %collective-permute-start.6 = (f32[400,128]{1,0:T(8,128)}, f32[400,128]{1,0:T(8,128)}, u32[]{:S(2)}, u32[]{:S(2)}) collective-permute-start(f32[400,128]{1,0:T(8,128)} %get-tuple-element.64), channel_id=1, source_target_pairs={{0,6},{1,7},{2,0},{3,1},{4,2},{5,3},{6,4},{7,5},{8,14},{9,15},{10,... | collective-permute-start | bytes 614408 | tf_op jit(solution)/shard_map/ppermute | solution.py:469
  33.3 1.9 %collective-permute-done.13.refs_2_ = f32[768,128]{1,0:T(8,128)S(1)} collective-permute-done((f32[768,128]{1,0:T(8,128)S(1)}, f32[768,128]{1,0:T(8,128)S(1)}, u32[]{:S(2)}, u32[]{:S(2)}) %collective-permute-start.13) | collective-permute-done | bytes 393248 | tf_op jit(solution)/shard_map/ppermute | solution.py:469
  35.1 1.9 %shard_map.97 = (f32[6,256,128]{2,1,0:T(8,128)S(1)}, f32[400,128]{1,0:T(8,128)}, f32[400,128]{1,0:T(8,128)}, f32[32,128]{1,0:T(8,128)S(1)}) custom-call(s32[1]{0:T(128)} %bitcast.refs_0_, f32[12,256,128]{2,1,0:T(8,128)S(1)} %bitcast.11, f32[768,128]{1,0:T(8,128)S(1)} %collective-permute-done.13.refs_2_, ...), custom_call_target="tpu_custom_call" | custom-call | flops 1024 | bytes 1024 | tf_op jit(solution)/shard_map/pallas_call | solution.py:435
  39.7 2.0 %collective-permute-start.15 = (f32[400,128]{1,0:T(8,128)}, f32[400,128]{1,0:T(8,128)}, u32[]{:S(2)}, u32[]{:S(2)}) collective-permute-start(f32[400,128]{1,0:T(8,128)} %get-tuple-element.83), channel_id=1, source_target_pairs={{0,6},{1,7},{2,0},{3,1},{4,2},{5,3},{6,4},{7,5},{8,14},{9,15},{10,... | collective-permute-start | bytes 614408 | tf_op jit(solution)/shard_map/ppermute | solution.py:469
  44.6 4.4 %shard_map.93 = (f32[6,256,128]{2,1,0:T(8,128)S(1)}, f32[400,128]{1,0:T(8,128)S(1)}, f32[400,128]{1,0:T(8,128)S(1)}, f32[32,128]{1,0:T(8,128)S(1)}) custom-call(f32[6,256,128]{2,1,0:T(8,128)S(1)} %copy-done.8, f32[400,128]{1,0:T(8,128)} %collective-permute-done.5.refs_1_, f32[400,128]{1,0:T(8,128)} %collective-permute-done.6.refs_2_, ...), custom_call_target="tpu_custom_call" | custom-call | flops 1024 | bytes 1024 | tf_op jit(solution)/shard_map/pallas_call | solution.py:435
  50.0 2.9 %collective-permute-start.8 = (f32[400,128]{1,0:T(8,128)S(1)}, f32[400,128]{1,0:T(8,128)S(1)}, u32[]{:S(2)}, u32[]{:S(2)}) collective-permute-start(f32[400,128]{1,0:T(8,128)S(1)} %get-tuple-element.70), channel_id=1, source_target_pairs={{0,6},{1,7},{2,0},{3,1},{4,2},{5,3},{6,4},{7,5},{8,14},{9,15},{10,... | collective-permute-start | bytes 614408 | tf_op jit(solution)/shard_map/ppermute | solution.py:469
  52.9 4.4 %shard_map.98 = (f32[6,256,128]{2,1,0:T(8,128)S(1)}, f32[400,128]{1,0:T(8,128)S(1)}, f32[400,128]{1,0:T(8,128)S(1)}, f32[32,128]{1,0:T(8,128)S(1)}) custom-call(f32[6,256,128]{2,1,0:T(8,128)S(1)} %copy-done.6, f32[400,128]{1,0:T(8,128)} %collective-permute-done.14.refs_1_, f32[400,128]{1,0:T(8,128)} %collective-permute-done.15.refs_2_, ...), custom_call_target="tpu_custom_call" | custom-call | flops 1024 | bytes 1024 | tf_op jit(solution)/shard_map/pallas_call | solution.py:435
  57.4 3.8 %collective-permute-start.17 = (f32[400,128]{1,0:T(8,128)S(1)}, f32[400,128]{1,0:T(8,128)S(1)}, u32[]{:S(2)}, u32[]{:S(2)}) collective-permute-start(f32[400,128]{1,0:T(8,128)S(1)} %get-tuple-element.87), channel_id=1, source_target_pairs={{0,6},{1,7},{2,0},{3,1},{4,2},{5,3},{6,4},{7,5},{8,14},{9,15},{10,... | collective-permute-start | bytes 614408 | tf_op jit(solution)/shard_map/ppermute | solution.py:469
  62.1 3.4 %shard_map.94 = (f32[6,256,128]{2,1,0:T(8,128)S(1)}, f32[400,128]{1,0:T(8,128)S(1)}, f32[400,128]{1,0:T(8,128)S(1)}, f32[32,128]{1,0:T(8,128)S(1)}) custom-call(f32[6,256,128]{2,1,0:T(8,128)S(1)} %get-tuple-element.68.refs_0_.refs_1_, f32[6,256,128]{2,1,0:T(8,128)S(1)} %copy-done.8, f32[400,128]{1,0:T(8,128)S(1)} %collective-permute-done.7.refs_2_, ...), custom_call_target="tpu_custom_call" | custom-call | flops 1024 | bytes 1024 | tf_op jit(solution)/shard_map/pallas_call | solution.py:435
  66.0 3.3 %collective-permute-start.10 = (f32[400,128]{1,0:T(8,128)S(1)}, f32[400,128]{1,0:T(8,128)S(1)}, u32[]{:S(2)}, u32[]{:S(2)}) collective-permute-start(f32[400,128]{1,0:T(8,128)S(1)} %get-tuple-element.74), channel_id=1, source_target_pairs={{0,6},{1,7},{2,0},{3,1},{4,2},{5,3},{6,4},{7,5},{8,14},{9,15},{10,... | collective-permute-start | bytes 614408 | tf_op jit(solution)/shard_map/ppermute | solution.py:469
  70.1 4.1 %shard_map.99 = (f32[6,256,128]{2,1,0:T(8,128)S(1)}, f32[400,128]{1,0:T(8,128)}, f32[400,128]{1,0:T(8,128)}, f32[32,128]{1,0:T(8,128)S(1)}) custom-call(f32[6,256,128]{2,1,0:T(8,128)S(1)} %get-tuple-element.85.refs_0_.refs_1_, f32[6,256,128]{2,1,0:T(8,128)S(1)} %copy-done.6, f32[400,128]{1,0:T(8,128)S(1)} %collective-permute-done.16.refs_2_, ...), custom_call_target="tpu_custom_call" | custom-call | flops 1024 | bytes 1024 | tf_op jit(solution)/shard_map/pallas_call | solution.py:435
  75.7 3.3 %collective-permute-start.19 = (f32[400,128]{1,0:T(8,128)}, f32[400,128]{1,0:T(8,128)}, u32[]{:S(2)}, u32[]{:S(2)}) collective-permute-start(f32[400,128]{1,0:T(8,128)} %get-tuple-element.91), channel_id=1, source_target_pairs={{0,6},{1,7},{2,0},{3,1},{4,2},{5,3},{6,4},{7,5},{8,14},{9,15},{10,... | collective-permute-start | bytes 614408 | tf_op jit(solution)/shard_map/ppermute | solution.py:469
  79.0 4.1 %shard_map.95 = (f32[6,256,128]{2,1,0:T(8,128)S(1)}, f32[400,128]{1,0:T(8,128)}, f32[400,128]{1,0:T(8,128)}, f32[32,128]{1,0:T(8,128)S(1)}) custom-call(f32[6,256,128]{2,1,0:T(8,128)S(1)} %get-tuple-element.72.refs_0_.refs_2_, f32[6,256,128]{2,1,0:T(8,128)S(1)} %get-tuple-element.68.refs_0_.refs_1_, f32[400,128]{1,0:T(8,128)S(1)} %collective-permute-done.9.refs_2_, ...), custom_call_target="tpu_custom_call" | custom-call | flops 1024 | bytes 1024 | tf_op jit(solution)/shard_map/pallas_call | solution.py:435
  84.1 3.7 %collective-permute-start.12 = (f32[400,128]{1,0:T(8,128)}, f32[400,128]{1,0:T(8,128)}, u32[]{:S(2)}, u32[]{:S(2)}) collective-permute-start(f32[400,128]{1,0:T(8,128)} %get-tuple-element.78), channel_id=1, source_target_pairs={{0,6},{1,7},{2,0},{3,1},{4,2},{5,3},{6,4},{7,5},{8,14},{9,15},{10,... | collective-permute-start | bytes 614408 | tf_op jit(solution)/shard_map/ppermute | solution.py:469
  90.8 4.5 %shard_map.100 = (f32[6,256,128]{2,1,0:T(8,128)S(1)}, f32[400,128]{1,0:T(8,128)S(1)}, f32[400,128]{1,0:T(8,128)S(1)}, f32[32,128]{1,0:T(8,128)S(1)}) custom-call(f32[6,256,128]{2,1,0:T(8,128)S(1)} %copy-done.10, f32[6,256,128]{2,1,0:T(8,128)S(1)} %copy-done.15, f32[400,128]{1,0:T(8,128)} %collective-permute-done.18.refs_2_, ...), custom_call_target="tpu_custom_call" | custom-call | flops 1024 | bytes 1024 | tf_op jit(solution)/shard_map/pallas_call | solution.py:435
  95.6 3.6 %collective-permute-start.21 = (f32[400,128]{1,0:T(8,128)S(1)}, f32[400,128]{1,0:T(8,128)S(1)}, u32[]{:S(2)}, u32[]{:S(2)}) collective-permute-start(f32[400,128]{1,0:T(8,128)S(1)} %get-tuple-element.95), channel_id=1, source_target_pairs={{0,6},{1,7},{2,0},{3,1},{4,2},{5,3},{6,4},{7,5},{8,14},{9,15},{10,... | collective-permute-start | bytes 614408 | tf_op jit(solution)/shard_map/ppermute | solution.py:469
  99.3 3.3 %shard_map.96 = (f32[384,128]{1,0:T(8,128)S(1)}, f32[384,128]{1,0:T(8,128)S(1)}, f32[384,128]{1,0:T(8,128)S(1)}, f32[384,128]{1,0:T(8,128)S(1)}) custom-call(s32[2]{0:T(128)S(1)} %pad_add_fusion.refs_0_, f32[6,256,128]{2,1,0:T(8,128)S(1)} %copy-done.17, f32[6,256,128]{2,1,0:T(8,128)S(1)} %copy-done.13, f32[400,128]{1,0:T(8,128)} %collective-permute-done.11.refs_3_, ...), custom_call_target="tpu_custom_call" | custom-call | flops 1024 | bytes 1024 | tf_op jit(solution)/shard_map/pallas_call | solution.py:435
  106.2 2.8 %shard_map.101 = (f32[384,128]{1,0:T(8,128)S(1)}, f32[384,128]{1,0:T(8,128)S(1)}, f32[384,128]{1,0:T(8,128)S(1)}, f32[384,128]{1,0:T(8,128)S(1)}) custom-call(s32[2]{0:T(128)S(1)} %pad_add_fusion.refs_0_, f32[6,256,128]{2,1,0:T(8,128)S(1)} %get-tuple-element.93.refs_1_, f32[6,256,128]{2,1,0:T(8,128)S(1)} %copy-done.11, ...), custom_call_target="tpu_custom_call" | custom-call | flops 1024 | bytes 1024 | tf_op jit(solution)/shard_map/pallas_call | solution.py:435
  113.3 2.4 %collective-permute-start.27 = (f32[384,128]{1,0:T(8,128)S(1)}, f32[384,128]{1,0:T(8,128)S(1)}, u32[]{:S(2)}, u32[]{:S(2)}) collective-permute-start(f32[384,128]{1,0:T(8,128)S(1)} %get-tuple-element.103.refs_6_), channel_id=1, source_target_pairs={{0,17},{1,16},{2,19},{3,18},{4,21},{5,20},{6,23},{7,22},{8,25},{9,... | collective-permute-start | bytes 589832 | tf_op jit(solution)/shard_map/ppermute | solution.py:493
  116.7 2.2 %collective-permute-done.23.refs_3_.refs_6_ = f32[384,128]{1,0:T(8,128)S(1)} collective-permute-done((f32[384,128]{1,0:T(8,128)S(1)}, f32[384,128]{1,0:T(8,128)S(1)}, u32[]{:S(2)}, u32[]{:S(2)}) %collective-permute-start.23) | collective-permute-done | bytes 196640 | tf_op jit(solution)/shard_map/ppermute | solution.py:469
  118.9 2.1 %collective-permute-done.27.refs_4_ = f32[384,128]{1,0:T(8,128)S(1)} collective-permute-done((f32[384,128]{1,0:T(8,128)S(1)}, f32[384,128]{1,0:T(8,128)S(1)}, u32[]{:S(2)}, u32[]{:S(2)}) %collective-permute-start.27) | collective-permute-done | bytes 196640 | tf_op jit(solution)/shard_map/ppermute | solution.py:493
  128.9 2.0 %collective-permute-done.30.refs_1_ = f32[64,512]{1,0:T(8,128)S(1)} collective-permute-done((f32[64,512]{1,0:T(8,128)S(1)}, f32[64,512]{1,0:T(8,128)S(1)}, u32[]{:S(2)}, u32[]{:S(2)}) %collective-permute-start.30) | collective-permute-done | bytes 131104 | tf_op jit(solution)/shard_map/ppermute | solution.py:469
  130.9 2.3 %collective-permute-done.31.refs_2_ = f32[64,512]{1,0:T(8,128)S(1)} collective-permute-done((f32[64,512]{1,0:T(8,128)S(1)}, f32[64,512]{1,0:T(8,128)S(1)}, u32[]{:S(2)}, u32[]{:S(2)}) %collective-permute-start.31) | collective-permute-done | bytes 131104 | tf_op jit(solution)/shard_map/ppermute | solution.py:469
  137.5 2.7 %collective-permute-start.36 = (f32[64,512]{1,0:T(8,128)S(1)}, f32[64,512]{1,0:T(8,128)S(1)}, u32[]{:S(2)}, u32[]{:S(2)}) collective-permute-start(f32[64,512]{1,0:T(8,128)S(1)} %shard_map.106.refs_1_), channel_id=1, source_target_pairs={{0,6},{1,7},{2,0},{3,1},{4,2},{5,3},{6,4},{7,5},{8,14},{9,15},{10,... | collective-permute-start | bytes 393224 | tf_op jit(solution)/shard_map/ppermute | solution.py:469
  140.3 4.5 %collective-permute-done.34.refs_2_ = f32[64,512]{1,0:T(8,128)S(1)} collective-permute-done((f32[64,512]{1,0:T(8,128)S(1)}, f32[64,512]{1,0:T(8,128)S(1)}, u32[]{:S(2)}, u32[]{:S(2)}) %collective-permute-start.34) | collective-permute-done | bytes 131104 | tf_op jit(solution)/shard_map/ppermute | solution.py:469
  144.7 3.4 %collective-permute-done.35.refs_3_ = f32[64,512]{1,0:T(8,128)S(1)} collective-permute-done((f32[64,512]{1,0:T(8,128)S(1)}, f32[64,512]{1,0:T(8,128)S(1)}, u32[]{:S(2)}, u32[]{:S(2)}) %collective-permute-start.35) | collective-permute-done | bytes 131104 | tf_op jit(solution)/shard_map/ppermute | solution.py:469
  149.4 3.4 %shard_map.107 = f32[12,256,128]{2,1,0:T(8,128)} custom-call(s32[2]{0:T(128)S(1)} %pad_add_fusion.refs_0_, f32[384,128]{1,0:T(8,128)S(1)} %get-tuple-element.80.refs_1_, f32[384,128]{1,0:T(8,128)S(1)} %copy-done.19, f32[384,128]{1,0:T(8,128)S(1)} %copy-done.22, f32[384,128]{1,0:T(8,128)S(1)} %copy-done.24, ...), custom_call_target="tpu_custom_call" | custom-call | flops 1024 | bytes 1024 | tf_op jit(solution)/shard_map/pallas_call | solution.py:435
  (133 shorter events, 51.4 us)
Async XLA Ops:
  2.5 14.7 %collective-permute-start = (f32[768,128]{1,0:T(8,128)S(1)}, f32[768,128]{1,0:T(8,128)S(1)}, u32[]{:S(2)}, u32[]{:S(2)}) collective-permute-start(f32[768,128]{1,0:T(8,128)S(1)} %shard_map.86.refs_4_), channel_id=1, source_target_pairs={{0,1},{1,0},{2,3},{3,2},{4,5},{5,4},{6,7},{7,6},{8,9},{9,8},{10,11... | collective-permute-start | bytes 1179656 | tf_op jit(solution)/shard_map/ppermute | solution.py:469
  7.5 16.0 %collective-permute-start.1 = (f32[19,16,256]{2,1,0:T(8,128)S(1)}, f32[19,16,256]{2,1,0:T(8,128)S(1)}, u32[]{:S(2)}, u32[]{:S(2)}) collective-permute-start(f32[19,16,256]{2,1,0:T(8,128)S(1)} %get-tuple-element.58), channel_id=1, source_target_pairs={{0,1},{1,0},{2,3},{3,2},{4,5},{5,4},{6,7},{7,6},{8,9},{9,8},{10,11... | collective-permute-start | bytes 933896 | tf_op jit(solution)/shard_map/ppermute | solution.py:469
  7.6 10.1 %collective-permute-start.2 = (f32[6,16,256]{2,1,0:T(8,128)S(1)}, f32[6,16,256]{2,1,0:T(8,128)S(1)}, u32[]{:S(2)}, u32[]{:S(2)}) collective-permute-start(f32[6,16,256]{2,1,0:T(8,128)S(1)} %get-tuple-element.59), channel_id=1, source_target_pairs={{0,6},{1,3},{2,0},{3,5},{4,2},{5,7},{6,4},{7,1},{8,14},{9,11},{10,... | collective-permute-start | bytes 294920 | tf_op jit(solution)/shard_map/ppermute | solution.py:469
  11.7 7.4 %collective-permute-start.3 = (f32[6,16,256]{2,1,0:T(8,128)S(1)}, f32[6,16,256]{2,1,0:T(8,128)S(1)}, u32[]{:S(2)}, u32[]{:S(2)}) collective-permute-start(f32[6,16,256]{2,1,0:T(8,128)S(1)} %get-tuple-element.59), channel_id=1, source_target_pairs={{0,7},{1,2},{2,1},{3,4},{4,3},{5,6},{6,5},{7,0},{8,15},{9,10},{10,... | collective-permute-start | bytes 294920 | tf_op jit(solution)/shard_map/ppermute | solution.py:469
  23.6 11.5 %collective-permute-start.13 = (f32[768,128]{1,0:T(8,128)S(1)}, f32[768,128]{1,0:T(8,128)S(1)}, u32[]{:S(2)}, u32[]{:S(2)}) collective-permute-start(f32[768,128]{1,0:T(8,128)S(1)} %shard_map.88.refs_4_), channel_id=1, source_target_pairs={{0,1},{1,0},{2,3},{3,2},{4,5},{5,4},{6,7},{7,6},{8,9},{9,8},{10,11... | collective-permute-start | bytes 1179656 | tf_op jit(solution)/shard_map/ppermute | solution.py:469
  29.3 12.5 %collective-permute-start.5 = (f32[400,128]{1,0:T(8,128)}, f32[400,128]{1,0:T(8,128)}, u32[]{:S(2)}, u32[]{:S(2)}) collective-permute-start(f32[400,128]{1,0:T(8,128)} %get-tuple-element.63), channel_id=1, source_target_pairs={{0,2},{1,3},{2,4},{3,5},{4,6},{5,7},{6,0},{7,1},{8,10},{9,11},{10,... | collective-permute-start | bytes 614408 | tf_op jit(solution)/shard_map/ppermute | solution.py:469
  31.1 12.3 %collective-permute-start.6 = (f32[400,128]{1,0:T(8,128)}, f32[400,128]{1,0:T(8,128)}, u32[]{:S(2)}, u32[]{:S(2)}) collective-permute-start(f32[400,128]{1,0:T(8,128)} %get-tuple-element.64), channel_id=1, source_target_pairs={{0,6},{1,7},{2,0},{3,1},{4,2},{5,3},{6,4},{7,5},{8,14},{9,15},{10,... | collective-permute-start | bytes 614408 | tf_op jit(solution)/shard_map/ppermute | solution.py:469
  37.9 15.0 %collective-permute-start.14 = (f32[400,128]{1,0:T(8,128)}, f32[400,128]{1,0:T(8,128)}, u32[]{:S(2)}, u32[]{:S(2)}) collective-permute-start(f32[400,128]{1,0:T(8,128)} %get-tuple-element.82), channel_id=1, source_target_pairs={{0,2},{1,3},{2,4},{3,5},{4,6},{5,7},{6,0},{7,1},{8,10},{9,11},{10,... | collective-permute-start | bytes 614408 | tf_op jit(solution)/shard_map/ppermute | solution.py:469
  39.7 13.2 %collective-permute-start.15 = (f32[400,128]{1,0:T(8,128)}, f32[400,128]{1,0:T(8,128)}, u32[]{:S(2)}, u32[]{:S(2)}) collective-permute-start(f32[400,128]{1,0:T(8,128)} %get-tuple-element.83), channel_id=1, source_target_pairs={{0,6},{1,7},{2,0},{3,1},{4,2},{5,3},{6,4},{7,5},{8,14},{9,15},{10,... | collective-permute-start | bytes 614408 | tf_op jit(solution)/shard_map/ppermute | solution.py:469
  49.1 12.1 %collective-permute-start.7 = (f32[400,128]{1,0:T(8,128)S(1)}, f32[400,128]{1,0:T(8,128)S(1)}, u32[]{:S(2)}, u32[]{:S(2)}) collective-permute-start(f32[400,128]{1,0:T(8,128)S(1)} %get-tuple-element.69), channel_id=1, source_target_pairs={{0,2},{1,3},{2,4},{3,5},{4,6},{5,7},{6,0},{7,1},{8,10},{9,11},{10,... | collective-permute-start | bytes 614408 | tf_op jit(solution)/shard_map/ppermute | solution.py:469
  50.0 12.1 %collective-permute-start.8 = (f32[400,128]{1,0:T(8,128)S(1)}, f32[400,128]{1,0:T(8,128)S(1)}, u32[]{:S(2)}, u32[]{:S(2)}) collective-permute-start(f32[400,128]{1,0:T(8,128)S(1)} %get-tuple-element.70), channel_id=1, source_target_pairs={{0,6},{1,7},{2,0},{3,1},{4,2},{5,3},{6,4},{7,5},{8,14},{9,15},{10,... | collective-permute-start | bytes 614408 | tf_op jit(solution)/shard_map/ppermute | solution.py:469
  57.3 12.1 %collective-permute-start.16 = (f32[400,128]{1,0:T(8,128)S(1)}, f32[400,128]{1,0:T(8,128)S(1)}, u32[]{:S(2)}, u32[]{:S(2)}) collective-permute-start(f32[400,128]{1,0:T(8,128)S(1)} %get-tuple-element.86), channel_id=1, source_target_pairs={{0,2},{1,3},{2,4},{3,5},{4,6},{5,7},{6,0},{7,1},{8,10},{9,11},{10,... | collective-permute-start | bytes 614408 | tf_op jit(solution)/shard_map/ppermute | solution.py:469
  57.4 12.8 %collective-permute-start.17 = (f32[400,128]{1,0:T(8,128)S(1)}, f32[400,128]{1,0:T(8,128)S(1)}, u32[]{:S(2)}, u32[]{:S(2)}) collective-permute-start(f32[400,128]{1,0:T(8,128)S(1)} %get-tuple-element.87), channel_id=1, source_target_pairs={{0,6},{1,7},{2,0},{3,1},{4,2},{5,3},{6,4},{7,5},{8,14},{9,15},{10,... | collective-permute-start | bytes 614408 | tf_op jit(solution)/shard_map/ppermute | solution.py:469
  65.5 13.5 %collective-permute-start.9 = (f32[400,128]{1,0:T(8,128)S(1)}, f32[400,128]{1,0:T(8,128)S(1)}, u32[]{:S(2)}, u32[]{:S(2)}) collective-permute-start(f32[400,128]{1,0:T(8,128)S(1)} %get-tuple-element.73), channel_id=1, source_target_pairs={{0,2},{1,3},{2,4},{3,5},{4,6},{5,7},{6,0},{7,1},{8,10},{9,11},{10,... | collective-permute-start | bytes 614408 | tf_op jit(solution)/shard_map/ppermute | solution.py:469
  66.0 13.0 %collective-permute-start.10 = (f32[400,128]{1,0:T(8,128)S(1)}, f32[400,128]{1,0:T(8,128)S(1)}, u32[]{:S(2)}, u32[]{:S(2)}) collective-permute-start(f32[400,128]{1,0:T(8,128)S(1)} %get-tuple-element.74), channel_id=1, source_target_pairs={{0,6},{1,7},{2,0},{3,1},{4,2},{5,3},{6,4},{7,5},{8,14},{9,15},{10,... | collective-permute-start | bytes 614408 | tf_op jit(solution)/shard_map/ppermute | solution.py:469
  75.2 12.7 %collective-permute-start.18 = (f32[400,128]{1,0:T(8,128)}, f32[400,128]{1,0:T(8,128)}, u32[]{:S(2)}, u32[]{:S(2)}) collective-permute-start(f32[400,128]{1,0:T(8,128)} %get-tuple-element.90), channel_id=1, source_target_pairs={{0,2},{1,3},{2,4},{3,5},{4,6},{5,7},{6,0},{7,1},{8,10},{9,11},{10,... | collective-permute-start | bytes 614408 | tf_op jit(solution)/shard_map/ppermute | solution.py:469
  75.7 12.9 %collective-permute-start.19 = (f32[400,128]{1,0:T(8,128)}, f32[400,128]{1,0:T(8,128)}, u32[]{:S(2)}, u32[]{:S(2)}) collective-permute-start(f32[400,128]{1,0:T(8,128)} %get-tuple-element.91), channel_id=1, source_target_pairs={{0,6},{1,7},{2,0},{3,1},{4,2},{5,3},{6,4},{7,5},{8,14},{9,15},{10,... | collective-permute-start | bytes 614408 | tf_op jit(solution)/shard_map/ppermute | solution.py:469
  84.0 15.3 %collective-permute-start.11 = (f32[400,128]{1,0:T(8,128)}, f32[400,128]{1,0:T(8,128)}, u32[]{:S(2)}, u32[]{:S(2)}) collective-permute-start(f32[400,128]{1,0:T(8,128)} %get-tuple-element.77), channel_id=1, source_target_pairs={{0,2},{1,3},{2,4},{3,5},{4,6},{5,7},{6,0},{7,1},{8,10},{9,11},{10,... | collective-permute-start | bytes 614408 | tf_op jit(solution)/shard_map/ppermute | solution.py:469
  84.1 15.2 %collective-permute-start.12 = (f32[400,128]{1,0:T(8,128)}, f32[400,128]{1,0:T(8,128)}, u32[]{:S(2)}, u32[]{:S(2)}) collective-permute-start(f32[400,128]{1,0:T(8,128)} %get-tuple-element.78), channel_id=1, source_target_pairs={{0,6},{1,7},{2,0},{3,1},{4,2},{5,3},{6,4},{7,5},{8,14},{9,15},{10,... | collective-permute-start | bytes 614408 | tf_op jit(solution)/shard_map/ppermute | solution.py:469
  95.4 10.9 %collective-permute-start.20 = (f32[400,128]{1,0:T(8,128)S(1)}, f32[400,128]{1,0:T(8,128)S(1)}, u32[]{:S(2)}, u32[]{:S(2)}) collective-permute-start(f32[400,128]{1,0:T(8,128)S(1)} %get-tuple-element.94), channel_id=1, source_target_pairs={{0,2},{1,3},{2,4},{3,5},{4,6},{5,7},{6,0},{7,1},{8,10},{9,11},{10,... | collective-permute-start | bytes 614408 | tf_op jit(solution)/shard_map/ppermute | solution.py:469
  95.6 10.6 %collective-permute-start.21 = (f32[400,128]{1,0:T(8,128)S(1)}, f32[400,128]{1,0:T(8,128)S(1)}, u32[]{:S(2)}, u32[]{:S(2)}) collective-permute-start(f32[400,128]{1,0:T(8,128)S(1)} %get-tuple-element.95), channel_id=1, source_target_pairs={{0,6},{1,7},{2,0},{3,1},{4,2},{5,3},{6,4},{7,5},{8,14},{9,15},{10,... | collective-permute-start | bytes 614408 | tf_op jit(solution)/shard_map/ppermute | solution.py:469
  102.7 10.6 %collective-permute-start.22 = (f32[384,128]{1,0:T(8,128)S(1)}, f32[384,128]{1,0:T(8,128)S(1)}, u32[]{:S(2)}, u32[]{:S(2)}) collective-permute-start(f32[384,128]{1,0:T(8,128)S(1)} %get-tuple-element.100), channel_id=1, source_target_pairs={{0,1},{1,0},{2,3},{3,2},{4,5},{5,4},{6,7},{7,6},{8,9},{9,8},{10,11... | collective-permute-start | bytes 589832 | tf_op jit(solution)/shard_map/ppermute | solution.py:469
  104.2 11.5 %collective-permute-start.24 = (f32[384,128]{1,0:T(8,128)S(1)}, f32[384,128]{1,0:T(8,128)S(1)}, u32[]{:S(2)}, u32[]{:S(2)}) collective-permute-start(f32[384,128]{1,0:T(8,128)S(1)} %get-tuple-element.98.refs_3_), channel_id=1, source_target_pairs={{0,16},{8,24},{16,0},{24,8},{1,17},{9,25},{17,1},{25,9},{2,18},{10... | collective-permute-start | bytes 589832 | tf_op jit(solution)/shard_map/ppermute | solution.py:469
  105.7 10.0 %collective-permute-start.25 = (f32[384,128]{1,0:T(8,128)S(1)}, f32[384,128]{1,0:T(8,128)S(1)}, u32[]{:S(2)}, u32[]{:S(2)}) collective-permute-start(f32[384,128]{1,0:T(8,128)S(1)} %get-tuple-element.102.refs_5_), channel_id=1, source_target_pairs={{0,17},{1,16},{2,19},{3,18},{4,21},{5,20},{6,23},{7,22},{8,25},{9,... | collective-permute-start | bytes 589832 | tf_op jit(solution)/shard_map/ppermute | solution.py:493
  109.0 9.8 %collective-permute-start.23 = (f32[384,128]{1,0:T(8,128)S(1)}, f32[384,128]{1,0:T(8,128)S(1)}, u32[]{:S(2)}, u32[]{:S(2)}) collective-permute-start(f32[384,128]{1,0:T(8,128)S(1)} %get-tuple-element.101), channel_id=1, source_target_pairs={{0,1},{1,0},{2,3},{3,2},{4,5},{5,4},{6,7},{7,6},{8,9},{9,8},{10,11... | collective-permute-start | bytes 589832 | tf_op jit(solution)/shard_map/ppermute | solution.py:469
  110.6 8.3 %collective-permute-start.26 = (f32[384,128]{1,0:T(8,128)S(1)}, f32[384,128]{1,0:T(8,128)S(1)}, u32[]{:S(2)}, u32[]{:S(2)}) collective-permute-start(f32[384,128]{1,0:T(8,128)S(1)} %get-tuple-element.99.refs_4_), channel_id=1, source_target_pairs={{0,16},{8,24},{16,0},{24,8},{1,17},{9,25},{17,1},{25,9},{2,18},{10... | collective-permute-start | bytes 589832 | tf_op jit(solution)/shard_map/ppermute | solution.py:469
  113.3 7.7 %collective-permute-start.27 = (f32[384,128]{1,0:T(8,128)S(1)}, f32[384,128]{1,0:T(8,128)S(1)}, u32[]{:S(2)}, u32[]{:S(2)}) collective-permute-start(f32[384,128]{1,0:T(8,128)S(1)} %get-tuple-element.103.refs_6_), channel_id=1, source_target_pairs={{0,17},{1,16},{2,19},{3,18},{4,21},{5,20},{6,23},{7,22},{8,25},{9,... | collective-permute-start | bytes 589832 | tf_op jit(solution)/shard_map/ppermute | solution.py:493
  128.3 6.6 %collective-permute-start.32 = (f32[64,512]{1,0:T(8,128)S(1)}, f32[64,512]{1,0:T(8,128)S(1)}, u32[]{:S(2)}, u32[]{:S(2)}) collective-permute-start(f32[64,512]{1,0:T(8,128)S(1)} %get-tuple-element.109), channel_id=1, source_target_pairs={{0,17},{1,16},{2,19},{3,18},{4,21},{5,20},{6,23},{7,22},{8,25},{9,... | collective-permute-start | bytes 393224 | tf_op jit(solution)/shard_map/ppermute | solution.py:493
  134.9 13.3 %collective-permute-start.33 = (f32[768,128]{1,0:T(8,128)S(1)}, f32[768,128]{1,0:T(8,128)S(1)}, u32[]{:S(2)}, u32[]{:S(2)}) collective-permute-start(f32[768,128]{1,0:T(8,128)S(1)} %get-tuple-element.110), channel_id=1, source_target_pairs={{0,1},{1,0},{2,3},{3,2},{4,5},{5,4},{6,7},{7,6},{8,9},{9,8},{10,11... | collective-permute-start | bytes 1179656 | tf_op jit(solution)/shard_map/ppermute | solution.py:469
  136.5 8.3 %collective-permute-start.34 = (f32[64,512]{1,0:T(8,128)S(1)}, f32[64,512]{1,0:T(8,128)S(1)}, u32[]{:S(2)}, u32[]{:S(2)}) collective-permute-start(f32[64,512]{1,0:T(8,128)S(1)} %shard_map.106.refs_1_), channel_id=1, source_target_pairs={{0,2},{1,3},{2,4},{3,5},{4,6},{5,7},{6,0},{7,1},{8,10},{9,11},{10,... | collective-permute-start | bytes 393224 | tf_op jit(solution)/shard_map/ppermute | solution.py:469
  136.5 11.7 %collective-permute-start.35 = (f32[64,512]{1,0:T(8,128)S(1)}, f32[64,512]{1,0:T(8,128)S(1)}, u32[]{:S(2)}, u32[]{:S(2)}) collective-permute-start(f32[64,512]{1,0:T(8,128)S(1)} %shard_map.106.refs_1_), channel_id=1, source_target_pairs={{0,4},{1,5},{2,6},{3,7},{4,0},{5,1},{6,2},{7,3},{8,12},{9,13},{10,... | collective-permute-start | bytes 393224 | tf_op jit(solution)/shard_map/ppermute | solution.py:469
  137.5 10.7 %collective-permute-start.36 = (f32[64,512]{1,0:T(8,128)S(1)}, f32[64,512]{1,0:T(8,128)S(1)}, u32[]{:S(2)}, u32[]{:S(2)}) collective-permute-start(f32[64,512]{1,0:T(8,128)S(1)} %shard_map.106.refs_1_), channel_id=1, source_target_pairs={{0,6},{1,7},{2,0},{3,1},{4,2},{5,3},{6,4},{7,5},{8,14},{9,15},{10,... | collective-permute-start | bytes 393224 | tf_op jit(solution)/shard_map/ppermute | solution.py:469
  (35 other events, 278.5 us)
where the time goes:
time: 155 us
  starting transfers between devices  60.1 us (39%)
  Pallas kernels  46.8 us (30%)
  waiting for transfers between devices  36.9 us (24%)
  local copies, waits for them, and re-layouts  9.65 us (6%)
    ppermute x35, starting transfers between devices, move(): lax.ppermute(array, axis, [(i, target(i) % size) for i in range(size)])  56.6 us
    pallas_call x24, Pallas kernels, call(): pl.pallas_call(body, out_shape=out, in_specs=[SMEM] * len(scalars) + [VME...  46.8 us
    ppermute x35, waiting for transfers between devices, move(): lax.ppermute(array, axis, [(i, target(i) % size) for i in range(size)])  33.1 us
    unnamed x58, local copies, waits for them, and re-layouts  8.51 us
    ppermute x3, waiting for transfers between devices, diagonal(): lax.ppermute(array, ('band', 'grid'), [(i, i ^ flip) for i in range(size)])  3.8 us
    ppermute x3, starting transfers between devices, diagonal(): lax.ppermute(array, ('band', 'grid'), [(i, i ^ flip) for i in range(size)])  3.45 us
  transfers between devices with their start and end apart: 38, of which 18 were waited for; matrix products, arithmetic and copies ran while one was open for 1% of the time, Pallas kernels for 28%

commit v1 on v0

--- a/solution.py
+++ b/solution.py
@@ -426,7 +426,7 @@
 ANY = pl.BlockSpec(memory_space=pl.ANY)
 
 
-def call(kernel, out, scalars, arrays, scratch=(), after=()):
+def call(kernel, out, scalars, arrays, scratch=(), after=(), cost=1 << 10):
     used = len(scalars) + len(arrays)
 
     def body(*refs):
@@ -439,7 +439,7 @@
         out_specs=[VMEM] * len(out),
         scratch_shapes=list(scratch),
         compiler_params=pltpu.CompilerParams(vmem_limit_bytes=16 * 1024 * 1024),
-        cost_estimate=pl.CostEstimate(flops=1 << 10, bytes_accessed=1 << 10, transcendentals=0),
+        cost_estimate=pl.CostEstimate(flops=cost, bytes_accessed=1 << 10, transcendentals=0),
     )(*scalars, *arrays, *after)
 
 
@@ -564,6 +564,7 @@
                 [yx] if last else [],
                 arrays,
                 [pltpu.VMEM((18, cells, LANES), F32)],
+                cost=1 << 30,
             )
             if last:
                 own, for_y, for_x, rest = made

time: 155 us -> 153 us (0.987)
    unnamed x58 -> x50, local copies, waits for them, and re-layouts: 8.51 us -> 7.56 us
  transfers between devices with their start and end apart: 38 -> 38, of which waited for: 18 -> 17; matrix products, arithmetic and copies ran while one was open for 1% -> 1% of each run, Pallas kernels for 28% -> 29%
where the time goes in v1:
time: 153 us
  starting transfers between devices  60.2 us (39%)
  Pallas kernels  47.3 us (31%)
  waiting for transfers between devices  35.6 us (23%)
  local copies, waits for them, and re-layouts  8.7 us (6%)
    ppermute x35, starting transfers between devices, move(): lax.ppermute(array, axis, [(i, target(i) % size) for i in range(size)])  56.9 us
    pallas_call x24, Pallas kernels, call(): pl.pallas_call(body, out_shape=out, in_specs=[SMEM] * len(scalars) + [VME...  47.3 us
    ppermute x35, waiting for transfers between devices, move(): lax.ppermute(array, axis, [(i, target(i) % size) for i in range(size)])  31.8 us
    unnamed x50, local copies, waits for them, and re-layouts  7.56 us
    ppermute x3, waiting for transfers between devices, diagonal(): lax.ppermute(array, ('band', 'grid'), [(i, i ^ flip) for i in range(size)])  3.81 us
    ppermute x3, starting transfers between devices, diagonal(): lax.ppermute(array, ('band', 'grid'), [(i, i ^ flip) for i in range(size)])  3.28 us
  transfers between devices with their start and end apart: 38, of which 17 were waited for; matrix products, arithmetic and copies ran while one was open for 1% of the time, Pallas kernels for 29%

profile of v1, /device:TPU:0, one launch (start us, length us, event | category | flops | bytes accessed | tf_op | source)
XLA Modules:
  0.0 153.0 jit_solution(18040096258525934874)
XLA Ops:
  2.5 3.0 %collective-permute-start = (f32[768,128]{1,0:T(8,128)S(1)}, f32[768,128]{1,0:T(8,128)S(1)}, u32[]{:S(2)}, u32[]{:S(2)}) collective-permute-start(f32[768,128]{1,0:T(8,128)S(1)} %shard_map.86.refs_4_), channel_id=1, source_target_pairs={{0,1},{1,0},{2,3},{3,2},{4,5},{5,4},{6,7},{7,6},{8,9},{9,8},{10,11... | collective-permute-start | bytes 1179656 | tf_op jit(solution)/shard_map/ppermute | solution.py:469
  7.6 4.1 %collective-permute-start.2 = (f32[6,16,256]{2,1,0:T(8,128)S(1)}, f32[6,16,256]{2,1,0:T(8,128)S(1)}, u32[]{:S(2)}, u32[]{:S(2)}) collective-permute-start(f32[6,16,256]{2,1,0:T(8,128)S(1)} %get-tuple-element.59), channel_id=1, source_target_pairs={{0,6},{1,3},{2,0},{3,5},{4,2},{5,7},{6,4},{7,1},{8,14},{9,11},{10,... | collective-permute-start | bytes 294920 | tf_op jit(solution)/shard_map/ppermute | solution.py:469
  12.9 4.4 %collective-permute-done.refs_2_ = f32[768,128]{1,0:T(8,128)S(1)} collective-permute-done((f32[768,128]{1,0:T(8,128)S(1)}, f32[768,128]{1,0:T(8,128)S(1)}, u32[]{:S(2)}, u32[]{:S(2)}) %collective-permute-start) | collective-permute-done | bytes 393248 | tf_op jit(solution)/shard_map/ppermute | solution.py:469
  19.1 4.4 %collective-permute-done.1.refs_1_.refs_2_ = f32[19,16,256]{2,1,0:T(8,128)S(1)} collective-permute-done((f32[19,16,256]{2,1,0:T(8,128)S(1)}, f32[19,16,256]{2,1,0:T(8,128)S(1)}, u32[]{:S(2)}, u32[]{:S(2)}) %collective-permute-start.1) | collective-permute-done | bytes 311328 | tf_op jit(solution)/shard_map/ppermute | solution.py:469
  26.5 1.9 %shard_map.91 = (f32[6,256,128]{2,1,0:T(8,128)S(1)}, f32[400,128]{1,0:T(8,128)}, f32[400,128]{1,0:T(8,128)}, f32[32,128]{1,0:T(8,128)S(1)}) custom-call(s32[1]{0:T(128)} %bitcast.refs_0_, f32[12,256,128]{2,1,0:T(8,128)S(1)} %bitcast.10, f32[768,128]{1,0:T(8,128)S(1)} %collective-permute-done.refs_2_, ...), custom_call_target="tpu_custom_call" | custom-call | flops 1024 | bytes 1024 | tf_op jit(solution)/shard_map/pallas_call | solution.py:435
  31.1 2.0 %collective-permute-start.6 = (f32[400,128]{1,0:T(8,128)}, f32[400,128]{1,0:T(8,128)}, u32[]{:S(2)}, u32[]{:S(2)}) collective-permute-start(f32[400,128]{1,0:T(8,128)} %get-tuple-element.64), channel_id=1, source_target_pairs={{0,6},{1,7},{2,0},{3,1},{4,2},{5,3},{6,4},{7,5},{8,14},{9,15},{10,... | collective-permute-start | bytes 614408 | tf_op jit(solution)/shard_map/ppermute | solution.py:469
  33.2 1.9 %collective-permute-done.13.refs_2_ = f32[768,128]{1,0:T(8,128)S(1)} collective-permute-done((f32[768,128]{1,0:T(8,128)S(1)}, f32[768,128]{1,0:T(8,128)S(1)}, u32[]{:S(2)}, u32[]{:S(2)}) %collective-permute-start.13) | collective-permute-done | bytes 393248 | tf_op jit(solution)/shard_map/ppermute | solution.py:469
  35.1 1.9 %shard_map.97 = (f32[6,256,128]{2,1,0:T(8,128)S(1)}, f32[400,128]{1,0:T(8,128)}, f32[400,128]{1,0:T(8,128)}, f32[32,128]{1,0:T(8,128)S(1)}) custom-call(s32[1]{0:T(128)} %bitcast.refs_0_, f32[12,256,128]{2,1,0:T(8,128)S(1)} %bitcast.11, f32[768,128]{1,0:T(8,128)S(1)} %collective-permute-done.13.refs_2_, ...), custom_call_target="tpu_custom_call" | custom-call | flops 1024 | bytes 1024 | tf_op jit(solution)/shard_map/pallas_call | solution.py:435
  39.7 2.0 %collective-permute-start.15 = (f32[400,128]{1,0:T(8,128)}, f32[400,128]{1,0:T(8,128)}, u32[]{:S(2)}, u32[]{:S(2)}) collective-permute-start(f32[400,128]{1,0:T(8,128)} %get-tuple-element.83), channel_id=1, source_target_pairs={{0,6},{1,7},{2,0},{3,1},{4,2},{5,3},{6,4},{7,5},{8,14},{9,15},{10,... | collective-permute-start | bytes 614408 | tf_op jit(solution)/shard_map/ppermute | solution.py:469
  44.6 4.4 %shard_map.93 = (f32[6,256,128]{2,1,0:T(8,128)S(1)}, f32[400,128]{1,0:T(8,128)S(1)}, f32[400,128]{1,0:T(8,128)S(1)}, f32[32,128]{1,0:T(8,128)S(1)}) custom-call(f32[6,256,128]{2,1,0:T(8,128)S(1)} %copy-done.8, f32[400,128]{1,0:T(8,128)} %collective-permute-done.5.refs_1_, f32[400,128]{1,0:T(8,128)} %collective-permute-done.6.refs_2_, ...), custom_call_target="tpu_custom_call" | custom-call | flops 1073741824 | bytes 1024 | tf_op jit(solution)/shard_map/pallas_call | solution.py:435
  50.0 2.9 %collective-permute-start.8 = (f32[400,128]{1,0:T(8,128)S(1)}, f32[400,128]{1,0:T(8,128)S(1)}, u32[]{:S(2)}, u32[]{:S(2)}) collective-permute-start(f32[400,128]{1,0:T(8,128)S(1)} %get-tuple-element.70), channel_id=1, source_target_pairs={{0,6},{1,7},{2,0},{3,1},{4,2},{5,3},{6,4},{7,5},{8,14},{9,15},{10,... | collective-permute-start | bytes 614408 | tf_op jit(solution)/shard_map/ppermute | solution.py:469
  52.9 4.4 %shard_map.98 = (f32[6,256,128]{2,1,0:T(8,128)S(1)}, f32[400,128]{1,0:T(8,128)S(1)}, f32[400,128]{1,0:T(8,128)S(1)}, f32[32,128]{1,0:T(8,128)S(1)}) custom-call(f32[6,256,128]{2,1,0:T(8,128)S(1)} %copy-done.6, f32[400,128]{1,0:T(8,128)} %collective-permute-done.14.refs_1_, f32[400,128]{1,0:T(8,128)} %collective-permute-done.15.refs_2_, ...), custom_call_target="tpu_custom_call" | custom-call | flops 1073741824 | bytes 1024 | tf_op jit(solution)/shard_map/pallas_call | solution.py:435
  57.4 3.8 %collective-permute-start.17 = (f32[400,128]{1,0:T(8,128)S(1)}, f32[400,128]{1,0:T(8,128)S(1)}, u32[]{:S(2)}, u32[]{:S(2)}) collective-permute-start(f32[400,128]{1,0:T(8,128)S(1)} %get-tuple-element.87), channel_id=1, source_target_pairs={{0,6},{1,7},{2,0},{3,1},{4,2},{5,3},{6,4},{7,5},{8,14},{9,15},{10,... | collective-permute-start | bytes 614408 | tf_op jit(solution)/shard_map/ppermute | solution.py:469
  62.1 4.2 %shard_map.94 = (f32[6,256,128]{2,1,0:T(8,128)S(1)}, f32[400,128]{1,0:T(8,128)}, f32[400,128]{1,0:T(8,128)}, f32[32,128]{1,0:T(8,128)S(1)}) custom-call(f32[6,256,128]{2,1,0:T(8,128)S(1)} %get-tuple-element.68.refs_0_.refs_1_, f32[6,256,128]{2,1,0:T(8,128)S(1)} %copy-done.8, f32[400,128]{1,0:T(8,128)S(1)} %collective-permute-done.7.refs_2_, ...), custom_call_target="tpu_custom_call" | custom-call | flops 1073741824 | bytes 1024 | tf_op jit(solution)/shard_map/pallas_call | solution.py:435
  66.8 3.3 %collective-permute-start.10 = (f32[400,128]{1,0:T(8,128)}, f32[400,128]{1,0:T(8,128)}, u32[]{:S(2)}, u32[]{:S(2)}) collective-permute-start(f32[400,128]{1,0:T(8,128)} %get-tuple-element.74), channel_id=1, source_target_pairs={{0,6},{1,7},{2,0},{3,1},{4,2},{5,3},{6,4},{7,5},{8,14},{9,15},{10,... | collective-permute-start | bytes 614408 | tf_op jit(solution)/shard_map/ppermute | solution.py:469
  70.1 4.1 %shard_map.99 = (f32[6,256,128]{2,1,0:T(8,128)S(1)}, f32[400,128]{1,0:T(8,128)}, f32[400,128]{1,0:T(8,128)}, f32[32,128]{1,0:T(8,128)S(1)}) custom-call(f32[6,256,128]{2,1,0:T(8,128)S(1)} %get-tuple-element.85.refs_0_.refs_1_, f32[6,256,128]{2,1,0:T(8,128)S(1)} %copy-done.6, f32[400,128]{1,0:T(8,128)S(1)} %collective-permute-done.16.refs_2_, ...), custom_call_target="tpu_custom_call" | custom-call | flops 1073741824 | bytes 1024 | tf_op jit(solution)/shard_map/pallas_call | solution.py:435
  75.4 3.6 %collective-permute-start.19 = (f32[400,128]{1,0:T(8,128)}, f32[400,128]{1,0:T(8,128)}, u32[]{:S(2)}, u32[]{:S(2)}) collective-permute-start(f32[400,128]{1,0:T(8,128)} %get-tuple-element.91), channel_id=1, source_target_pairs={{0,6},{1,7},{2,0},{3,1},{4,2},{5,3},{6,4},{7,5},{8,14},{9,15},{10,... | collective-permute-start | bytes 614408 | tf_op jit(solution)/shard_map/ppermute | solution.py:469
  81.8 4.5 %shard_map.95 = (f32[6,256,128]{2,1,0:T(8,128)S(1)}, f32[400,128]{1,0:T(8,128)S(1)}, f32[400,128]{1,0:T(8,128)S(1)}, f32[32,128]{1,0:T(8,128)S(1)}) custom-call(f32[6,256,128]{2,1,0:T(8,128)S(1)} %copy-done.16, f32[6,256,128]{2,1,0:T(8,128)S(1)} %copy-done.12, f32[400,128]{1,0:T(8,128)} %collective-permute-done.9.refs_2_, ...), custom_call_target="tpu_custom_call" | custom-call | flops 1073741824 | bytes 1024 | tf_op jit(solution)/shard_map/pallas_call | solution.py:435
  86.8 3.3 %collective-permute-start.12 = (f32[400,128]{1,0:T(8,128)S(1)}, f32[400,128]{1,0:T(8,128)S(1)}, u32[]{:S(2)}, u32[]{:S(2)}) collective-permute-start(f32[400,128]{1,0:T(8,128)S(1)} %get-tuple-element.78), channel_id=1, source_target_pairs={{0,6},{1,7},{2,0},{3,1},{4,2},{5,3},{6,4},{7,5},{8,14},{9,15},{10,... | collective-permute-start | bytes 614408 | tf_op jit(solution)/shard_map/ppermute | solution.py:469
  90.2 4.5 %shard_map.100 = (f32[6,256,128]{2,1,0:T(8,128)S(1)}, f32[400,128]{1,0:T(8,128)S(1)}, f32[400,128]{1,0:T(8,128)S(1)}, f32[32,128]{1,0:T(8,128)S(1)}) custom-call(f32[6,256,128]{2,1,0:T(8,128)S(1)} %copy-done.14, f32[6,256,128]{2,1,0:T(8,128)S(1)} %copy-done.10, f32[400,128]{1,0:T(8,128)} %collective-permute-done.18.refs_2_, ...), custom_call_target="tpu_custom_call" | custom-call | flops 1073741824 | bytes 1024 | tf_op jit(solution)/shard_map/pallas_call | solution.py:435
  94.7 3.8 %collective-permute-start.21 = (f32[400,128]{1,0:T(8,128)S(1)}, f32[400,128]{1,0:T(8,128)S(1)}, u32[]{:S(2)}, u32[]{:S(2)}) collective-permute-start(f32[400,128]{1,0:T(8,128)S(1)} %get-tuple-element.95), channel_id=1, source_target_pairs={{0,6},{1,7},{2,0},{3,1},{4,2},{5,3},{6,4},{7,5},{8,14},{9,15},{10,... | collective-permute-start | bytes 614408 | tf_op jit(solution)/shard_map/ppermute | solution.py:469
  98.6 2.8 %shard_map.96 = (f32[384,128]{1,0:T(8,128)S(1)}, f32[384,128]{1,0:T(8,128)S(1)}, f32[384,128]{1,0:T(8,128)S(1)}, f32[384,128]{1,0:T(8,128)S(1)}) custom-call(s32[2]{0:T(128)S(1)} %pad_add_fusion.refs_0_, f32[6,256,128]{2,1,0:T(8,128)S(1)} %get-tuple-element.76.refs_1_, f32[6,256,128]{2,1,0:T(8,128)S(1)} %copy-done.17, ...), custom_call_target="tpu_custom_call" | custom-call | flops 1073741824 | bytes 1024 | tf_op jit(solution)/shard_map/pallas_call | solution.py:435
  104.9 2.8 %shard_map.101 = (f32[384,128]{1,0:T(8,128)S(1)}, f32[384,128]{1,0:T(8,128)S(1)}, f32[384,128]{1,0:T(8,128)S(1)}, f32[384,128]{1,0:T(8,128)S(1)}) custom-call(s32[2]{0:T(128)S(1)} %pad_add_fusion.refs_0_, f32[6,256,128]{2,1,0:T(8,128)S(1)} %get-tuple-element.93.refs_1_, f32[6,256,128]{2,1,0:T(8,128)S(1)} %copy-done.14, ...), custom_call_target="tpu_custom_call" | custom-call | flops 1073741824 | bytes 1024 | tf_op jit(solution)/shard_map/pallas_call | solution.py:435
  111.4 2.3 %collective-permute-start.27 = (f32[384,128]{1,0:T(8,128)S(1)}, f32[384,128]{1,0:T(8,128)S(1)}, u32[]{:S(2)}, u32[]{:S(2)}) collective-permute-start(f32[384,128]{1,0:T(8,128)S(1)} %get-tuple-element.103.refs_6_), channel_id=1, source_target_pairs={{0,17},{1,16},{2,19},{3,18},{4,21},{5,20},{6,23},{7,22},{8,25},{9,... | collective-permute-start | bytes 589832 | tf_op jit(solution)/shard_map/ppermute | solution.py:493
  114.7 2.7 %collective-permute-done.23.refs_3_.refs_6_ = f32[384,128]{1,0:T(8,128)S(1)} collective-permute-done((f32[384,128]{1,0:T(8,128)S(1)}, f32[384,128]{1,0:T(8,128)S(1)}, u32[]{:S(2)}, u32[]{:S(2)}) %collective-permute-start.23) | collective-permute-done | bytes 196640 | tf_op jit(solution)/shard_map/ppermute | solution.py:469
  117.4 2.1 %collective-permute-done.27.refs_4_ = f32[384,128]{1,0:T(8,128)S(1)} collective-permute-done((f32[384,128]{1,0:T(8,128)S(1)}, f32[384,128]{1,0:T(8,128)S(1)}, u32[]{:S(2)}, u32[]{:S(2)}) %collective-permute-start.27) | collective-permute-done | bytes 196640 | tf_op jit(solution)/shard_map/ppermute | solution.py:493
  127.3 2.0 %collective-permute-done.30.refs_1_ = f32[64,512]{1,0:T(8,128)S(1)} collective-permute-done((f32[64,512]{1,0:T(8,128)S(1)}, f32[64,512]{1,0:T(8,128)S(1)}, u32[]{:S(2)}, u32[]{:S(2)}) %collective-permute-start.30) | collective-permute-done | bytes 131104 | tf_op jit(solution)/shard_map/ppermute | solution.py:469
  129.3 2.3 %collective-permute-done.31.refs_2_ = f32[64,512]{1,0:T(8,128)S(1)} collective-permute-done((f32[64,512]{1,0:T(8,128)S(1)}, f32[64,512]{1,0:T(8,128)S(1)}, u32[]{:S(2)}, u32[]{:S(2)}) %collective-permute-start.31) | collective-permute-done | bytes 131104 | tf_op jit(solution)/shard_map/ppermute | solution.py:469
  135.3 2.0 %collective-permute-start.35 = (f32[64,512]{1,0:T(8,128)S(1)}, f32[64,512]{1,0:T(8,128)S(1)}, u32[]{:S(2)}, u32[]{:S(2)}) collective-permute-start(f32[64,512]{1,0:T(8,128)S(1)} %shard_map.106.refs_1_), channel_id=1, source_target_pairs={{0,4},{1,5},{2,6},{3,7},{4,0},{5,1},{6,2},{7,3},{8,12},{9,13},{10,... | collective-permute-start | bytes 393224 | tf_op jit(solution)/shard_map/ppermute | solution.py:469
  138.8 4.4 %collective-permute-done.34.refs_2_ = f32[64,512]{1,0:T(8,128)S(1)} collective-permute-done((f32[64,512]{1,0:T(8,128)S(1)}, f32[64,512]{1,0:T(8,128)S(1)}, u32[]{:S(2)}, u32[]{:S(2)}) %collective-permute-start.34) | collective-permute-done | bytes 131104 | tf_op jit(solution)/shard_map/ppermute | solution.py:469
  143.2 3.4 %collective-permute-done.35.refs_3_ = f32[64,512]{1,0:T(8,128)S(1)} collective-permute-done((f32[64,512]{1,0:T(8,128)S(1)}, f32[64,512]{1,0:T(8,128)S(1)}, u32[]{:S(2)}, u32[]{:S(2)}) %collective-permute-start.35) | collective-permute-done | bytes 131104 | tf_op jit(solution)/shard_map/ppermute | solution.py:469
  147.8 3.4 %shard_map.107 = f32[12,256,128]{2,1,0:T(8,128)} custom-call(s32[2]{0:T(128)S(1)} %pad_add_fusion.refs_0_, f32[384,128]{1,0:T(8,128)S(1)} %get-tuple-element.80.refs_1_, f32[384,128]{1,0:T(8,128)S(1)} %get-tuple-element.97.refs_1_.refs_2_, f32[384,128]{1,0:T(8,128)S(1)} %get-tuple-element.98.refs_3_, f32[384,128]{1,0:T(8,128)S(1)} %copy-done.20, ...), custom_call_target="tpu_custom_call" | custom-call | flops 1024 | bytes 1024 | tf_op jit(solution)/shard_map/pallas_call | solution.py:435
  (125 shorter events, 49.6 us)
Async XLA Ops:
  2.5 14.7 %collective-permute-start = (f32[768,128]{1,0:T(8,128)S(1)}, f32[768,128]{1,0:T(8,128)S(1)}, u32[]{:S(2)}, u32[]{:S(2)}) collective-permute-start(f32[768,128]{1,0:T(8,128)S(1)} %shard_map.86.refs_4_), channel_id=1, source_target_pairs={{0,1},{1,0},{2,3},{3,2},{4,5},{5,4},{6,7},{7,6},{8,9},{9,8},{10,11... | collective-permute-start | bytes 1179656 | tf_op jit(solution)/shard_map/ppermute | solution.py:469
  7.5 16.0 %collective-permute-start.1 = (f32[19,16,256]{2,1,0:T(8,128)S(1)}, f32[19,16,256]{2,1,0:T(8,128)S(1)}, u32[]{:S(2)}, u32[]{:S(2)}) collective-permute-start(f32[19,16,256]{2,1,0:T(8,128)S(1)} %get-tuple-element.58), channel_id=1, source_target_pairs={{0,1},{1,0},{2,3},{3,2},{4,5},{5,4},{6,7},{7,6},{8,9},{9,8},{10,11... | collective-permute-start | bytes 933896 | tf_op jit(solution)/shard_map/ppermute | solution.py:469
  7.6 10.1 %collective-permute-start.2 = (f32[6,16,256]{2,1,0:T(8,128)S(1)}, f32[6,16,256]{2,1,0:T(8,128)S(1)}, u32[]{:S(2)}, u32[]{:S(2)}) collective-permute-start(f32[6,16,256]{2,1,0:T(8,128)S(1)} %get-tuple-element.59), channel_id=1, source_target_pairs={{0,6},{1,3},{2,0},{3,5},{4,2},{5,7},{6,4},{7,1},{8,14},{9,11},{10,... | collective-permute-start | bytes 294920 | tf_op jit(solution)/shard_map/ppermute | solution.py:469
  11.7 7.4 %collective-permute-start.3 = (f32[6,16,256]{2,1,0:T(8,128)S(1)}, f32[6,16,256]{2,1,0:T(8,128)S(1)}, u32[]{:S(2)}, u32[]{:S(2)}) collective-permute-start(f32[6,16,256]{2,1,0:T(8,128)S(1)} %get-tuple-element.59), channel_id=1, source_target_pairs={{0,7},{1,2},{2,1},{3,4},{4,3},{5,6},{6,5},{7,0},{8,15},{9,10},{10,... | collective-permute-start | bytes 294920 | tf_op jit(solution)/shard_map/ppermute | solution.py:469
  23.6 11.5 %collective-permute-start.13 = (f32[768,128]{1,0:T(8,128)S(1)}, f32[768,128]{1,0:T(8,128)S(1)}, u32[]{:S(2)}, u32[]{:S(2)}) collective-permute-start(f32[768,128]{1,0:T(8,128)S(1)} %shard_map.88.refs_4_), channel_id=1, source_target_pairs={{0,1},{1,0},{2,3},{3,2},{4,5},{5,4},{6,7},{7,6},{8,9},{9,8},{10,11... | collective-permute-start | bytes 1179656 | tf_op jit(solution)/shard_map/ppermute | solution.py:469
  29.3 12.5 %collective-permute-start.5 = (f32[400,128]{1,0:T(8,128)}, f32[400,128]{1,0:T(8,128)}, u32[]{:S(2)}, u32[]{:S(2)}) collective-permute-start(f32[400,128]{1,0:T(8,128)} %get-tuple-element.63), channel_id=1, source_target_pairs={{0,2},{1,3},{2,4},{3,5},{4,6},{5,7},{6,0},{7,1},{8,10},{9,11},{10,... | collective-permute-start | bytes 614408 | tf_op jit(solution)/shard_map/ppermute | solution.py:469
  31.1 12.3 %collective-permute-start.6 = (f32[400,128]{1,0:T(8,128)}, f32[400,128]{1,0:T(8,128)}, u32[]{:S(2)}, u32[]{:S(2)}) collective-permute-start(f32[400,128]{1,0:T(8,128)} %get-tuple-element.64), channel_id=1, source_target_pairs={{0,6},{1,7},{2,0},{3,1},{4,2},{5,3},{6,4},{7,5},{8,14},{9,15},{10,... | collective-permute-start | bytes 614408 | tf_op jit(solution)/shard_map/ppermute | solution.py:469
  37.9 15.0 %collective-permute-start.14 = (f32[400,128]{1,0:T(8,128)}, f32[400,128]{1,0:T(8,128)}, u32[]{:S(2)}, u32[]{:S(2)}) collective-permute-start(f32[400,128]{1,0:T(8,128)} %get-tuple-element.82), channel_id=1, source_target_pairs={{0,2},{1,3},{2,4},{3,5},{4,6},{5,7},{6,0},{7,1},{8,10},{9,11},{10,... | collective-permute-start | bytes 614408 | tf_op jit(solution)/shard_map/ppermute | solution.py:469
  39.7 13.3 %collective-permute-start.15 = (f32[400,128]{1,0:T(8,128)}, f32[400,128]{1,0:T(8,128)}, u32[]{:S(2)}, u32[]{:S(2)}) collective-permute-start(f32[400,128]{1,0:T(8,128)} %get-tuple-element.83), channel_id=1, source_target_pairs={{0,6},{1,7},{2,0},{3,1},{4,2},{5,3},{6,4},{7,5},{8,14},{9,15},{10,... | collective-permute-start | bytes 614408 | tf_op jit(solution)/shard_map/ppermute | solution.py:469
  49.1 12.1 %collective-permute-start.7 = (f32[400,128]{1,0:T(8,128)S(1)}, f32[400,128]{1,0:T(8,128)S(1)}, u32[]{:S(2)}, u32[]{:S(2)}) collective-permute-start(f32[400,128]{1,0:T(8,128)S(1)} %get-tuple-element.69), channel_id=1, source_target_pairs={{0,2},{1,3},{2,4},{3,5},{4,6},{5,7},{6,0},{7,1},{8,10},{9,11},{10,... | collective-permute-start | bytes 614408 | tf_op jit(solution)/shard_map/ppermute | solution.py:469
  50.0 12.1 %collective-permute-start.8 = (f32[400,128]{1,0:T(8,128)S(1)}, f32[400,128]{1,0:T(8,128)S(1)}, u32[]{:S(2)}, u32[]{:S(2)}) collective-permute-start(f32[400,128]{1,0:T(8,128)S(1)} %get-tuple-element.70), channel_id=1, source_target_pairs={{0,6},{1,7},{2,0},{3,1},{4,2},{5,3},{6,4},{7,5},{8,14},{9,15},{10,... | collective-permute-start | bytes 614408 | tf_op jit(solution)/shard_map/ppermute | solution.py:469
  57.3 12.8 %collective-permute-start.16 = (f32[400,128]{1,0:T(8,128)S(1)}, f32[400,128]{1,0:T(8,128)S(1)}, u32[]{:S(2)}, u32[]{:S(2)}) collective-permute-start(f32[400,128]{1,0:T(8,128)S(1)} %get-tuple-element.86), channel_id=1, source_target_pairs={{0,2},{1,3},{2,4},{3,5},{4,6},{5,7},{6,0},{7,1},{8,10},{9,11},{10,... | collective-permute-start | bytes 614408 | tf_op jit(solution)/shard_map/ppermute | solution.py:469
  57.4 12.8 %collective-permute-start.17 = (f32[400,128]{1,0:T(8,128)S(1)}, f32[400,128]{1,0:T(8,128)S(1)}, u32[]{:S(2)}, u32[]{:S(2)}) collective-permute-start(f32[400,128]{1,0:T(8,128)S(1)} %get-tuple-element.87), channel_id=1, source_target_pairs={{0,6},{1,7},{2,0},{3,1},{4,2},{5,3},{6,4},{7,5},{8,14},{9,15},{10,... | collective-permute-start | bytes 614408 | tf_op jit(solution)/shard_map/ppermute | solution.py:469
  66.3 12.7 %collective-permute-start.9 = (f32[400,128]{1,0:T(8,128)}, f32[400,128]{1,0:T(8,128)}, u32[]{:S(2)}, u32[]{:S(2)}) collective-permute-start(f32[400,128]{1,0:T(8,128)} %get-tuple-element.73), channel_id=1, source_target_pairs={{0,2},{1,3},{2,4},{3,5},{4,6},{5,7},{6,0},{7,1},{8,10},{9,11},{10,... | collective-permute-start | bytes 614408 | tf_op jit(solution)/shard_map/ppermute | solution.py:469
  66.8 12.7 %collective-permute-start.10 = (f32[400,128]{1,0:T(8,128)}, f32[400,128]{1,0:T(8,128)}, u32[]{:S(2)}, u32[]{:S(2)}) collective-permute-start(f32[400,128]{1,0:T(8,128)} %get-tuple-element.74), channel_id=1, source_target_pairs={{0,6},{1,7},{2,0},{3,1},{4,2},{5,3},{6,4},{7,5},{8,14},{9,15},{10,... | collective-permute-start | bytes 614408 | tf_op jit(solution)/shard_map/ppermute | solution.py:469
  75.2 15.0 %collective-permute-start.18 = (f32[400,128]{1,0:T(8,128)}, f32[400,128]{1,0:T(8,128)}, u32[]{:S(2)}, u32[]{:S(2)}) collective-permute-start(f32[400,128]{1,0:T(8,128)} %get-tuple-element.90), channel_id=1, source_target_pairs={{0,2},{1,3},{2,4},{3,5},{4,6},{5,7},{6,0},{7,1},{8,10},{9,11},{10,... | collective-permute-start | bytes 614408 | tf_op jit(solution)/shard_map/ppermute | solution.py:469
  75.4 14.8 %collective-permute-start.19 = (f32[400,128]{1,0:T(8,128)}, f32[400,128]{1,0:T(8,128)}, u32[]{:S(2)}, u32[]{:S(2)}) collective-permute-start(f32[400,128]{1,0:T(8,128)} %get-tuple-element.91), channel_id=1, source_target_pairs={{0,6},{1,7},{2,0},{3,1},{4,2},{5,3},{6,4},{7,5},{8,14},{9,15},{10,... | collective-permute-start | bytes 614408 | tf_op jit(solution)/shard_map/ppermute | solution.py:469
  86.3 12.3 %collective-permute-start.11 = (f32[400,128]{1,0:T(8,128)S(1)}, f32[400,128]{1,0:T(8,128)S(1)}, u32[]{:S(2)}, u32[]{:S(2)}) collective-permute-start(f32[400,128]{1,0:T(8,128)S(1)} %get-tuple-element.77), channel_id=1, source_target_pairs={{0,2},{1,3},{2,4},{3,5},{4,6},{5,7},{6,0},{7,1},{8,10},{9,11},{10,... | collective-permute-start | bytes 614408 | tf_op jit(solution)/shard_map/ppermute | solution.py:469
  86.8 11.8 %collective-permute-start.12 = (f32[400,128]{1,0:T(8,128)S(1)}, f32[400,128]{1,0:T(8,128)S(1)}, u32[]{:S(2)}, u32[]{:S(2)}) collective-permute-start(f32[400,128]{1,0:T(8,128)S(1)} %get-tuple-element.78), channel_id=1, source_target_pairs={{0,6},{1,7},{2,0},{3,1},{4,2},{5,3},{6,4},{7,5},{8,14},{9,15},{10,... | collective-permute-start | bytes 614408 | tf_op jit(solution)/shard_map/ppermute | solution.py:469
  94.7 10.3 %collective-permute-start.20 = (f32[400,128]{1,0:T(8,128)S(1)}, f32[400,128]{1,0:T(8,128)S(1)}, u32[]{:S(2)}, u32[]{:S(2)}) collective-permute-start(f32[400,128]{1,0:T(8,128)S(1)} %get-tuple-element.94), channel_id=1, source_target_pairs={{0,2},{1,3},{2,4},{3,5},{4,6},{5,7},{6,0},{7,1},{8,10},{9,11},{10,... | collective-permute-start | bytes 614408 | tf_op jit(solution)/shard_map/ppermute | solution.py:469
  94.7 10.2 %collective-permute-start.21 = (f32[400,128]{1,0:T(8,128)S(1)}, f32[400,128]{1,0:T(8,128)S(1)}, u32[]{:S(2)}, u32[]{:S(2)}) collective-permute-start(f32[400,128]{1,0:T(8,128)S(1)} %get-tuple-element.95), channel_id=1, source_target_pairs={{0,6},{1,7},{2,0},{3,1},{4,2},{5,3},{6,4},{7,5},{8,14},{9,15},{10,... | collective-permute-start | bytes 614408 | tf_op jit(solution)/shard_map/ppermute | solution.py:469
  101.4 10.0 %collective-permute-start.22 = (f32[384,128]{1,0:T(8,128)S(1)}, f32[384,128]{1,0:T(8,128)S(1)}, u32[]{:S(2)}, u32[]{:S(2)}) collective-permute-start(f32[384,128]{1,0:T(8,128)S(1)} %get-tuple-element.100), channel_id=1, source_target_pairs={{0,1},{1,0},{2,3},{3,2},{4,5},{5,4},{6,7},{7,6},{8,9},{9,8},{10,11... | collective-permute-start | bytes 589832 | tf_op jit(solution)/shard_map/ppermute | solution.py:469
  103.0 10.7 %collective-permute-start.24 = (f32[384,128]{1,0:T(8,128)S(1)}, f32[384,128]{1,0:T(8,128)S(1)}, u32[]{:S(2)}, u32[]{:S(2)}) collective-permute-start(f32[384,128]{1,0:T(8,128)S(1)} %get-tuple-element.98.refs_3_), channel_id=1, source_target_pairs={{0,16},{8,24},{16,0},{24,8},{1,17},{9,25},{17,1},{25,9},{2,18},{10... | collective-permute-start | bytes 589832 | tf_op jit(solution)/shard_map/ppermute | solution.py:469
  104.5 9.2 %collective-permute-start.25 = (f32[384,128]{1,0:T(8,128)S(1)}, f32[384,128]{1,0:T(8,128)S(1)}, u32[]{:S(2)}, u32[]{:S(2)}) collective-permute-start(f32[384,128]{1,0:T(8,128)S(1)} %get-tuple-element.102.refs_5_), channel_id=1, source_target_pairs={{0,17},{1,16},{2,19},{3,18},{4,21},{5,20},{6,23},{7,22},{8,25},{9,... | collective-permute-start | bytes 589832 | tf_op jit(solution)/shard_map/ppermute | solution.py:493
  107.7 9.6 %collective-permute-start.23 = (f32[384,128]{1,0:T(8,128)S(1)}, f32[384,128]{1,0:T(8,128)S(1)}, u32[]{:S(2)}, u32[]{:S(2)}) collective-permute-start(f32[384,128]{1,0:T(8,128)S(1)} %get-tuple-element.101), channel_id=1, source_target_pairs={{0,1},{1,0},{2,3},{3,2},{4,5},{5,4},{6,7},{7,6},{8,9},{9,8},{10,11... | collective-permute-start | bytes 589832 | tf_op jit(solution)/shard_map/ppermute | solution.py:469
  109.4 8.0 %collective-permute-start.26 = (f32[384,128]{1,0:T(8,128)S(1)}, f32[384,128]{1,0:T(8,128)S(1)}, u32[]{:S(2)}, u32[]{:S(2)}) collective-permute-start(f32[384,128]{1,0:T(8,128)S(1)} %get-tuple-element.99.refs_4_), channel_id=1, source_target_pairs={{0,16},{8,24},{16,0},{24,8},{1,17},{9,25},{17,1},{25,9},{2,18},{10... | collective-permute-start | bytes 589832 | tf_op jit(solution)/shard_map/ppermute | solution.py:469
  111.4 8.1 %collective-permute-start.27 = (f32[384,128]{1,0:T(8,128)S(1)}, f32[384,128]{1,0:T(8,128)S(1)}, u32[]{:S(2)}, u32[]{:S(2)}) collective-permute-start(f32[384,128]{1,0:T(8,128)S(1)} %get-tuple-element.103.refs_6_), channel_id=1, source_target_pairs={{0,17},{1,16},{2,19},{3,18},{4,21},{5,20},{6,23},{7,22},{8,25},{9,... | collective-permute-start | bytes 589832 | tf_op jit(solution)/shard_map/ppermute | solution.py:493
  126.8 6.6 %collective-permute-start.32 = (f32[64,512]{1,0:T(8,128)S(1)}, f32[64,512]{1,0:T(8,128)S(1)}, u32[]{:S(2)}, u32[]{:S(2)}) collective-permute-start(f32[64,512]{1,0:T(8,128)S(1)} %get-tuple-element.109), channel_id=1, source_target_pairs={{0,17},{1,16},{2,19},{3,18},{4,21},{5,20},{6,23},{7,22},{8,25},{9,... | collective-permute-start | bytes 393224 | tf_op jit(solution)/shard_map/ppermute | solution.py:493
  133.4 13.3 %collective-permute-start.33 = (f32[768,128]{1,0:T(8,128)S(1)}, f32[768,128]{1,0:T(8,128)S(1)}, u32[]{:S(2)}, u32[]{:S(2)}) collective-permute-start(f32[768,128]{1,0:T(8,128)S(1)} %get-tuple-element.110), channel_id=1, source_target_pairs={{0,1},{1,0},{2,3},{3,2},{4,5},{5,4},{6,7},{7,6},{8,9},{9,8},{10,11... | collective-permute-start | bytes 1179656 | tf_op jit(solution)/shard_map/ppermute | solution.py:469
  134.9 8.3 %collective-permute-start.34 = (f32[64,512]{1,0:T(8,128)S(1)}, f32[64,512]{1,0:T(8,128)S(1)}, u32[]{:S(2)}, u32[]{:S(2)}) collective-permute-start(f32[64,512]{1,0:T(8,128)S(1)} %shard_map.106.refs_1_), channel_id=1, source_target_pairs={{0,2},{1,3},{2,4},{3,5},{4,6},{5,7},{6,0},{7,1},{8,10},{9,11},{10,... | collective-permute-start | bytes 393224 | tf_op jit(solution)/shard_map/ppermute | solution.py:469
  135.3 11.3 %collective-permute-start.35 = (f32[64,512]{1,0:T(8,128)S(1)}, f32[64,512]{1,0:T(8,128)S(1)}, u32[]{:S(2)}, u32[]{:S(2)}) collective-permute-start(f32[64,512]{1,0:T(8,128)S(1)} %shard_map.106.refs_1_), channel_id=1, source_target_pairs={{0,4},{1,5},{2,6},{3,7},{4,0},{5,1},{6,2},{7,3},{8,12},{9,13},{10,... | collective-permute-start | bytes 393224 | tf_op jit(solution)/shard_map/ppermute | solution.py:469
  137.3 9.3 %collective-permute-start.36 = (f32[64,512]{1,0:T(8,128)S(1)}, f32[64,512]{1,0:T(8,128)S(1)}, u32[]{:S(2)}, u32[]{:S(2)}) collective-permute-start(f32[64,512]{1,0:T(8,128)S(1)} %shard_map.106.refs_1_), channel_id=1, source_target_pairs={{0,6},{1,7},{2,0},{3,1},{4,2},{5,3},{6,4},{7,5},{8,14},{9,15},{10,... | collective-permute-start | bytes 393224 | tf_op jit(solution)/shard_map/ppermute | solution.py:469
  (31 other events, 217.2 us)

commit v2 on v1

--- a/solution.py
+++ b/solution.py
@@ -564,7 +564,7 @@
                 [yx] if last else [],
                 arrays,
                 [pltpu.VMEM((18, cells, LANES), F32)],
-                cost=1 << 30,
+                cost=1 << 29,
             )
             if last:
                 own, for_y, for_x, rest = made

time: 153 us -> 155 us (1.013)
    unnamed x50 -> x58, local copies, waits for them, and re-layouts: 7.56 us -> 8.51 us
  transfers between devices with their start and end apart: 38 -> 38, of which waited for: 17 -> 18; matrix products, arithmetic and copies ran while one was open for 1% -> 1% of each run, Pallas kernels for 29% -> 28%
where the time goes in v2:
time: 155 us
  starting transfers between devices  60.1 us (39%)
  Pallas kernels  46.8 us (30%)
  waiting for transfers between devices  36.9 us (24%)
  local copies, waits for them, and re-layouts  9.65 us (6%)
    ppermute x35, starting transfers between devices, move(): lax.ppermute(array, axis, [(i, target(i) % size) for i in range(size)])  56.6 us
    pallas_call x24, Pallas kernels, call(): pl.pallas_call(body, out_shape=out, in_specs=[SMEM] * len(scalars) + [VME...  46.8 us
    ppermute x35, waiting for transfers between devices, move(): lax.ppermute(array, axis, [(i, target(i) % size) for i in range(size)])  33.1 us
    unnamed x58, local copies, waits for them, and re-layouts  8.51 us
    ppermute x3, waiting for transfers between devices, diagonal(): lax.ppermute(array, ('band', 'grid'), [(i, i ^ flip) for i in range(size)])  3.8 us
    ppermute x3, starting transfers between devices, diagonal(): lax.ppermute(array, ('band', 'grid'), [(i, i ^ flip) for i in range(size)])  3.45 us
  transfers between devices with their start and end apart: 38, of which 18 were waited for; matrix products, arithmetic and copies ran while one was open for 1% of the time, Pallas kernels for 28%

profile of v2, /device:TPU:0, one launch (start us, length us, event | category | flops | bytes accessed | tf_op | source)
XLA Modules:
  0.0 154.6 jit_solution(1287880534524184717)
XLA Ops:
  2.5 3.0 %collective-permute-start = (f32[768,128]{1,0:T(8,128)S(1)}, f32[768,128]{1,0:T(8,128)S(1)}, u32[]{:S(2)}, u32[]{:S(2)}) collective-permute-start(f32[768,128]{1,0:T(8,128)S(1)} %shard_map.86.refs_4_), channel_id=1, source_target_pairs={{0,1},{1,0},{2,3},{3,2},{4,5},{5,4},{6,7},{7,6},{8,9},{9,8},{10,11... | collective-permute-start | bytes 1179656 | tf_op jit(solution)/shard_map/ppermute | solution.py:469
  7.6 4.1 %collective-permute-start.2 = (f32[6,16,256]{2,1,0:T(8,128)S(1)}, f32[6,16,256]{2,1,0:T(8,128)S(1)}, u32[]{:S(2)}, u32[]{:S(2)}) collective-permute-start(f32[6,16,256]{2,1,0:T(8,128)S(1)} %get-tuple-element.59), channel_id=1, source_target_pairs={{0,6},{1,3},{2,0},{3,5},{4,2},{5,7},{6,4},{7,1},{8,14},{9,11},{10,... | collective-permute-start | bytes 294920 | tf_op jit(solution)/shard_map/ppermute | solution.py:469
  12.9 4.4 %collective-permute-done.refs_2_ = f32[768,128]{1,0:T(8,128)S(1)} collective-permute-done((f32[768,128]{1,0:T(8,128)S(1)}, f32[768,128]{1,0:T(8,128)S(1)}, u32[]{:S(2)}, u32[]{:S(2)}) %collective-permute-start) | collective-permute-done | bytes 393248 | tf_op jit(solution)/shard_map/ppermute | solution.py:469
  19.1 4.4 %collective-permute-done.1.refs_1_.refs_2_ = f32[19,16,256]{2,1,0:T(8,128)S(1)} collective-permute-done((f32[19,16,256]{2,1,0:T(8,128)S(1)}, f32[19,16,256]{2,1,0:T(8,128)S(1)}, u32[]{:S(2)}, u32[]{:S(2)}) %collective-permute-start.1) | collective-permute-done | bytes 311328 | tf_op jit(solution)/shard_map/ppermute | solution.py:469
  26.5 1.9 %shard_map.91 = (f32[6,256,128]{2,1,0:T(8,128)S(1)}, f32[400,128]{1,0:T(8,128)}, f32[400,128]{1,0:T(8,128)}, f32[32,128]{1,0:T(8,128)S(1)}) custom-call(s32[1]{0:T(128)} %bitcast.refs_0_, f32[12,256,128]{2,1,0:T(8,128)S(1)} %bitcast.10, f32[768,128]{1,0:T(8,128)S(1)} %collective-permute-done.refs_2_, ...), custom_call_target="tpu_custom_call" | custom-call | flops 1024 | bytes 1024 | tf_op jit(solution)/shard_map/pallas_call | solution.py:435
  31.1 2.0 %collective-permute-start.6 = (f32[400,128]{1,0:T(8,128)}, f32[400,128]{1,0:T(8,128)}, u32[]{:S(2)}, u32[]{:S(2)}) collective-permute-start(f32[400,128]{1,0:T(8,128)} %get-tuple-element.64), channel_id=1, source_target_pairs={{0,6},{1,7},{2,0},{3,1},{4,2},{5,3},{6,4},{7,5},{8,14},{9,15},{10,... | collective-permute-start | bytes 614408 | tf_op jit(solution)/shard_map/ppermute | solution.py:469
  33.3 1.9 %collective-permute-done.13.refs_2_ = f32[768,128]{1,0:T(8,128)S(1)} collective-permute-done((f32[768,128]{1,0:T(8,128)S(1)}, f32[768,128]{1,0:T(8,128)S(1)}, u32[]{:S(2)}, u32[]{:S(2)}) %collective-permute-start.13) | collective-permute-done | bytes 393248 | tf_op jit(solution)/shard_map/ppermute | solution.py:469
  35.1 1.9 %shard_map.97 = (f32[6,256,128]{2,1,0:T(8,128)S(1)}, f32[400,128]{1,0:T(8,128)}, f32[400,128]{1,0:T(8,128)}, f32[32,128]{1,0:T(8,128)S(1)}) custom-call(s32[1]{0:T(128)} %bitcast.refs_0_, f32[12,256,128]{2,1,0:T(8,128)S(1)} %bitcast.11, f32[768,128]{1,0:T(8,128)S(1)} %collective-permute-done.13.refs_2_, ...), custom_call_target="tpu_custom_call" | custom-call | flops 1024 | bytes 1024 | tf_op jit(solution)/shard_map/pallas_call | solution.py:435
  39.7 2.0 %collective-permute-start.15 = (f32[400,128]{1,0:T(8,128)}, f32[400,128]{1,0:T(8,128)}, u32[]{:S(2)}, u32[]{:S(2)}) collective-permute-start(f32[400,128]{1,0:T(8,128)} %get-tuple-element.83), channel_id=1, source_target_pairs={{0,6},{1,7},{2,0},{3,1},{4,2},{5,3},{6,4},{7,5},{8,14},{9,15},{10,... | collective-permute-start | bytes 614408 | tf_op jit(solution)/shard_map/ppermute | solution.py:469
  44.6 4.4 %shard_map.93 = (f32[6,256,128]{2,1,0:T(8,128)S(1)}, f32[400,128]{1,0:T(8,128)S(1)}, f32[400,128]{1,0:T(8,128)S(1)}, f32[32,128]{1,0:T(8,128)S(1)}) custom-call(f32[6,256,128]{2,1,0:T(8,128)S(1)} %copy-done.8, f32[400,128]{1,0:T(8,128)} %collective-permute-done.5.refs_1_, f32[400,128]{1,0:T(8,128)} %collective-permute-done.6.refs_2_, ...), custom_call_target="tpu_custom_call" | custom-call | flops 536870912 | bytes 1024 | tf_op jit(solution)/shard_map/pallas_call | solution.py:435
  50.0 2.9 %collective-permute-start.8 = (f32[400,128]{1,0:T(8,128)S(1)}, f32[400,128]{1,0:T(8,128)S(1)}, u32[]{:S(2)}, u32[]{:S(2)}) collective-permute-start(f32[400,128]{1,0:T(8,128)S(1)} %get-tuple-element.70), channel_id=1, source_target_pairs={{0,6},{1,7},{2,0},{3,1},{4,2},{5,3},{6,4},{7,5},{8,14},{9,15},{10,... | collective-permute-start | bytes 614408 | tf_op jit(solution)/shard_map/ppermute | solution.py:469
  52.9 4.4 %shard_map.98 = (f32[6,256,128]{2,1,0:T(8,128)S(1)}, f32[400,128]{1,0:T(8,128)S(1)}, f32[400,128]{1,0:T(8,128)S(1)}, f32[32,128]{1,0:T(8,128)S(1)}) custom-call(f32[6,256,128]{2,1,0:T(8,128)S(1)} %copy-done.6, f32[400,128]{1,0:T(8,128)} %collective-permute-done.14.refs_1_, f32[400,128]{1,0:T(8,128)} %collective-permute-done.15.refs_2_, ...), custom_call_target="tpu_custom_call" | custom-call | flops 536870912 | bytes 1024 | tf_op jit(solution)/shard_map/pallas_call | solution.py:435
  57.4 3.8 %collective-permute-start.17 = (f32[400,128]{1,0:T(8,128)S(1)}, f32[400,128]{1,0:T(8,128)S(1)}, u32[]{:S(2)}, u32[]{:S(2)}) collective-permute-start(f32[400,128]{1,0:T(8,128)S(1)} %get-tuple-element.87), channel_id=1, source_target_pairs={{0,6},{1,7},{2,0},{3,1},{4,2},{5,3},{6,4},{7,5},{8,14},{9,15},{10,... | collective-permute-start | bytes 614408 | tf_op jit(solution)/shard_map/ppermute | solution.py:469
  62.1 3.4 %shard_map.94 = (f32[6,256,128]{2,1,0:T(8,128)S(1)}, f32[400,128]{1,0:T(8,128)S(1)}, f32[400,128]{1,0:T(8,128)S(1)}, f32[32,128]{1,0:T(8,128)S(1)}) custom-call(f32[6,256,128]{2,1,0:T(8,128)S(1)} %get-tuple-element.68.refs_0_.refs_1_, f32[6,256,128]{2,1,0:T(8,128)S(1)} %copy-done.8, f32[400,128]{1,0:T(8,128)S(1)} %collective-permute-done.7.refs_2_, ...), custom_call_target="tpu_custom_call" | custom-call | flops 536870912 | bytes 1024 | tf_op jit(solution)/shard_map/pallas_call | solution.py:435
  66.0 3.3 %collective-permute-start.10 = (f32[400,128]{1,0:T(8,128)S(1)}, f32[400,128]{1,0:T(8,128)S(1)}, u32[]{:S(2)}, u32[]{:S(2)}) collective-permute-start(f32[400,128]{1,0:T(8,128)S(1)} %get-tuple-element.74), channel_id=1, source_target_pairs={{0,6},{1,7},{2,0},{3,1},{4,2},{5,3},{6,4},{7,5},{8,14},{9,15},{10,... | collective-permute-start | bytes 614408 | tf_op jit(solution)/shard_map/ppermute | solution.py:469
  70.1 4.1 %shard_map.99 = (f32[6,256,128]{2,1,0:T(8,128)S(1)}, f32[400,128]{1,0:T(8,128)}, f32[400,128]{1,0:T(8,128)}, f32[32,128]{1,0:T(8,128)S(1)}) custom-call(f32[6,256,128]{2,1,0:T(8,128)S(1)} %get-tuple-element.85.refs_0_.refs_1_, f32[6,256,128]{2,1,0:T(8,128)S(1)} %copy-done.6, f32[400,128]{1,0:T(8,128)S(1)} %collective-permute-done.16.refs_2_, ...), custom_call_target="tpu_custom_call" | custom-call | flops 536870912 | bytes 1024 | tf_op jit(solution)/shard_map/pallas_call | solution.py:435
  75.7 3.3 %collective-permute-start.19 = (f32[400,128]{1,0:T(8,128)}, f32[400,128]{1,0:T(8,128)}, u32[]{:S(2)}, u32[]{:S(2)}) collective-permute-start(f32[400,128]{1,0:T(8,128)} %get-tuple-element.91), channel_id=1, source_target_pairs={{0,6},{1,7},{2,0},{3,1},{4,2},{5,3},{6,4},{7,5},{8,14},{9,15},{10,... | collective-permute-start | bytes 614408 | tf_op jit(solution)/shard_map/ppermute | solution.py:469
  79.0 4.1 %shard_map.95 = (f32[6,256,128]{2,1,0:T(8,128)S(1)}, f32[400,128]{1,0:T(8,128)}, f32[400,128]{1,0:T(8,128)}, f32[32,128]{1,0:T(8,128)S(1)}) custom-call(f32[6,256,128]{2,1,0:T(8,128)S(1)} %get-tuple-element.72.refs_0_.refs_2_, f32[6,256,128]{2,1,0:T(8,128)S(1)} %get-tuple-element.68.refs_0_.refs_1_, f32[400,128]{1,0:T(8,128)S(1)} %collective-permute-done.9.refs_2_, ...), custom_call_target="tpu_custom_call" | custom-call | flops 536870912 | bytes 1024 | tf_op jit(solution)/shard_map/pallas_call | solution.py:435
  84.1 3.7 %collective-permute-start.12 = (f32[400,128]{1,0:T(8,128)}, f32[400,128]{1,0:T(8,128)}, u32[]{:S(2)}, u32[]{:S(2)}) collective-permute-start(f32[400,128]{1,0:T(8,128)} %get-tuple-element.78), channel_id=1, source_target_pairs={{0,6},{1,7},{2,0},{3,1},{4,2},{5,3},{6,4},{7,5},{8,14},{9,15},{10,... | collective-permute-start | bytes 614408 | tf_op jit(solution)/shard_map/ppermute | solution.py:469
  90.8 4.5 %shard_map.100 = (f32[6,256,128]{2,1,0:T(8,128)S(1)}, f32[400,128]{1,0:T(8,128)S(1)}, f32[400,128]{1,0:T(8,128)S(1)}, f32[32,128]{1,0:T(8,128)S(1)}) custom-call(f32[6,256,128]{2,1,0:T(8,128)S(1)} %copy-done.10, f32[6,256,128]{2,1,0:T(8,128)S(1)} %copy-done.15, f32[400,128]{1,0:T(8,128)} %collective-permute-done.18.refs_2_, ...), custom_call_target="tpu_custom_call" | custom-call | flops 536870912 | bytes 1024 | tf_op jit(solution)/shard_map/pallas_call | solution.py:435
  95.6 3.6 %collective-permute-start.21 = (f32[400,128]{1,0:T(8,128)S(1)}, f32[400,128]{1,0:T(8,128)S(1)}, u32[]{:S(2)}, u32[]{:S(2)}) collective-permute-start(f32[400,128]{1,0:T(8,128)S(1)} %get-tuple-element.95), channel_id=1, source_target_pairs={{0,6},{1,7},{2,0},{3,1},{4,2},{5,3},{6,4},{7,5},{8,14},{9,15},{10,... | collective-permute-start | bytes 614408 | tf_op jit(solution)/shard_map/ppermute | solution.py:469
  99.3 3.3 %shard_map.96 = (f32[384,128]{1,0:T(8,128)S(1)}, f32[384,128]{1,0:T(8,128)S(1)}, f32[384,128]{1,0:T(8,128)S(1)}, f32[384,128]{1,0:T(8,128)S(1)}) custom-call(s32[2]{0:T(128)S(1)} %pad_add_fusion.refs_0_, f32[6,256,128]{2,1,0:T(8,128)S(1)} %copy-done.17, f32[6,256,128]{2,1,0:T(8,128)S(1)} %copy-done.13, f32[400,128]{1,0:T(8,128)} %collective-permute-done.11.refs_3_, ...), custom_call_target="tpu_custom_call" | custom-call | flops 536870912 | bytes 1024 | tf_op jit(solution)/shard_map/pallas_call | solution.py:435
  106.2 2.8 %shard_map.101 = (f32[384,128]{1,0:T(8,128)S(1)}, f32[384,128]{1,0:T(8,128)S(1)}, f32[384,128]{1,0:T(8,128)S(1)}, f32[384,128]{1,0:T(8,128)S(1)}) custom-call(s32[2]{0:T(128)S(1)} %pad_add_fusion.refs_0_, f32[6,256,128]{2,1,0:T(8,128)S(1)} %get-tuple-element.93.refs_1_, f32[6,256,128]{2,1,0:T(8,128)S(1)} %copy-done.11, ...), custom_call_target="tpu_custom_call" | custom-call | flops 536870912 | bytes 1024 | tf_op jit(solution)/shard_map/pallas_call | solution.py:435
  113.3 2.4 %collective-permute-start.27 = (f32[384,128]{1,0:T(8,128)S(1)}, f32[384,128]{1,0:T(8,128)S(1)}, u32[]{:S(2)}, u32[]{:S(2)}) collective-permute-start(f32[384,128]{1,0:T(8,128)S(1)} %get-tuple-element.103.refs_6_), channel_id=1, source_target_pairs={{0,17},{1,16},{2,19},{3,18},{4,21},{5,20},{6,23},{7,22},{8,25},{9,... | collective-permute-start | bytes 589832 | tf_op jit(solution)/shard_map/ppermute | solution.py:493
  116.7 2.2 %collective-permute-done.23.refs_3_.refs_6_ = f32[384,128]{1,0:T(8,128)S(1)} collective-permute-done((f32[384,128]{1,0:T(8,128)S(1)}, f32[384,128]{1,0:T(8,128)S(1)}, u32[]{:S(2)}, u32[]{:S(2)}) %collective-permute-start.23) | collective-permute-done | bytes 196640 | tf_op jit(solution)/shard_map/ppermute | solution.py:469
  118.9 2.1 %collective-permute-done.27.refs_4_ = f32[384,128]{1,0:T(8,128)S(1)} collective-permute-done((f32[384,128]{1,0:T(8,128)S(1)}, f32[384,128]{1,0:T(8,128)S(1)}, u32[]{:S(2)}, u32[]{:S(2)}) %collective-permute-start.27) | collective-permute-done | bytes 196640 | tf_op jit(solution)/shard_map/ppermute | solution.py:493
  128.9 2.0 %collective-permute-done.30.refs_1_ = f32[64,512]{1,0:T(8,128)S(1)} collective-permute-done((f32[64,512]{1,0:T(8,128)S(1)}, f32[64,512]{1,0:T(8,128)S(1)}, u32[]{:S(2)}, u32[]{:S(2)}) %collective-permute-start.30) | collective-permute-done | bytes 131104 | tf_op jit(solution)/shard_map/ppermute | solution.py:469
  130.9 2.3 %collective-permute-done.31.refs_2_ = f32[64,512]{1,0:T(8,128)S(1)} collective-permute-done((f32[64,512]{1,0:T(8,128)S(1)}, f32[64,512]{1,0:T(8,128)S(1)}, u32[]{:S(2)}, u32[]{:S(2)}) %collective-permute-start.31) | collective-permute-done | bytes 131104 | tf_op jit(solution)/shard_map/ppermute | solution.py:469
  137.5 2.7 %collective-permute-start.36 = (f32[64,512]{1,0:T(8,128)S(1)}, f32[64,512]{1,0:T(8,128)S(1)}, u32[]{:S(2)}, u32[]{:S(2)}) collective-permute-start(f32[64,512]{1,0:T(8,128)S(1)} %shard_map.106.refs_1_), channel_id=1, source_target_pairs={{0,6},{1,7},{2,0},{3,1},{4,2},{5,3},{6,4},{7,5},{8,14},{9,15},{10,... | collective-permute-start | bytes 393224 | tf_op jit(solution)/shard_map/ppermute | solution.py:469
  140.3 4.5 %collective-permute-done.34.refs_2_ = f32[64,512]{1,0:T(8,128)S(1)} collective-permute-done((f32[64,512]{1,0:T(8,128)S(1)}, f32[64,512]{1,0:T(8,128)S(1)}, u32[]{:S(2)}, u32[]{:S(2)}) %collective-permute-start.34) | collective-permute-done | bytes 131104 | tf_op jit(solution)/shard_map/ppermute | solution.py:469
  144.7 3.4 %collective-permute-done.35.refs_3_ = f32[64,512]{1,0:T(8,128)S(1)} collective-permute-done((f32[64,512]{1,0:T(8,128)S(1)}, f32[64,512]{1,0:T(8,128)S(1)}, u32[]{:S(2)}, u32[]{:S(2)}) %collective-permute-start.35) | collective-permute-done | bytes 131104 | tf_op jit(solution)/shard_map/ppermute | solution.py:469
  149.4 3.4 %shard_map.107 = f32[12,256,128]{2,1,0:T(8,128)} custom-call(s32[2]{0:T(128)S(1)} %pad_add_fusion.refs_0_, f32[384,128]{1,0:T(8,128)S(1)} %get-tuple-element.80.refs_1_, f32[384,128]{1,0:T(8,128)S(1)} %copy-done.19, f32[384,128]{1,0:T(8,128)S(1)} %copy-done.22, f32[384,128]{1,0:T(8,128)S(1)} %copy-done.24, ...), custom_call_target="tpu_custom_call" | custom-call | flops 1024 | bytes 1024 | tf_op jit(solution)/shard_map/pallas_call | solution.py:435
  (133 shorter events, 51.4 us)
Async XLA Ops:
  2.5 14.7 %collective-permute-start = (f32[768,128]{1,0:T(8,128)S(1)}, f32[768,128]{1,0:T(8,128)S(1)}, u32[]{:S(2)}, u32[]{:S(2)}) collective-permute-start(f32[768,128]{1,0:T(8,128)S(1)} %shard_map.86.refs_4_), channel_id=1, source_target_pairs={{0,1},{1,0},{2,3},{3,2},{4,5},{5,4},{6,7},{7,6},{8,9},{9,8},{10,11... | collective-permute-start | bytes 1179656 | tf_op jit(solution)/shard_map/ppermute | solution.py:469
  7.5 16.0 %collective-permute-start.1 = (f32[19,16,256]{2,1,0:T(8,128)S(1)}, f32[19,16,256]{2,1,0:T(8,128)S(1)}, u32[]{:S(2)}, u32[]{:S(2)}) collective-permute-start(f32[19,16,256]{2,1,0:T(8,128)S(1)} %get-tuple-element.58), channel_id=1, source_target_pairs={{0,1},{1,0},{2,3},{3,2},{4,5},{5,4},{6,7},{7,6},{8,9},{9,8},{10,11... | collective-permute-start | bytes 933896 | tf_op jit(solution)/shard_map/ppermute | solution.py:469
  7.6 10.1 %collective-permute-start.2 = (f32[6,16,256]{2,1,0:T(8,128)S(1)}, f32[6,16,256]{2,1,0:T(8,128)S(1)}, u32[]{:S(2)}, u32[]{:S(2)}) collective-permute-start(f32[6,16,256]{2,1,0:T(8,128)S(1)} %get-tuple-element.59), channel_id=1, source_target_pairs={{0,6},{1,3},{2,0},{3,5},{4,2},{5,7},{6,4},{7,1},{8,14},{9,11},{10,... | collective-permute-start | bytes 294920 | tf_op jit(solution)/shard_map/ppermute | solution.py:469
  11.7 7.4 %collective-permute-start.3 = (f32[6,16,256]{2,1,0:T(8,128)S(1)}, f32[6,16,256]{2,1,0:T(8,128)S(1)}, u32[]{:S(2)}, u32[]{:S(2)}) collective-permute-start(f32[6,16,256]{2,1,0:T(8,128)S(1)} %get-tuple-element.59), channel_id=1, source_target_pairs={{0,7},{1,2},{2,1},{3,4},{4,3},{5,6},{6,5},{7,0},{8,15},{9,10},{10,... | collective-permute-start | bytes 294920 | tf_op jit(solution)/shard_map/ppermute | solution.py:469
  23.6 11.5 %collective-permute-start.13 = (f32[768,128]{1,0:T(8,128)S(1)}, f32[768,128]{1,0:T(8,128)S(1)}, u32[]{:S(2)}, u32[]{:S(2)}) collective-permute-start(f32[768,128]{1,0:T(8,128)S(1)} %shard_map.88.refs_4_), channel_id=1, source_target_pairs={{0,1},{1,0},{2,3},{3,2},{4,5},{5,4},{6,7},{7,6},{8,9},{9,8},{10,11... | collective-permute-start | bytes 1179656 | tf_op jit(solution)/shard_map/ppermute | solution.py:469
  29.3 12.5 %collective-permute-start.5 = (f32[400,128]{1,0:T(8,128)}, f32[400,128]{1,0:T(8,128)}, u32[]{:S(2)}, u32[]{:S(2)}) collective-permute-start(f32[400,128]{1,0:T(8,128)} %get-tuple-element.63), channel_id=1, source_target_pairs={{0,2},{1,3},{2,4},{3,5},{4,6},{5,7},{6,0},{7,1},{8,10},{9,11},{10,... | collective-permute-start | bytes 614408 | tf_op jit(solution)/shard_map/ppermute | solution.py:469
  31.1 12.3 %collective-permute-start.6 = (f32[400,128]{1,0:T(8,128)}, f32[400,128]{1,0:T(8,128)}, u32[]{:S(2)}, u32[]{:S(2)}) collective-permute-start(f32[400,128]{1,0:T(8,128)} %get-tuple-element.64), channel_id=1, source_target_pairs={{0,6},{1,7},{2,0},{3,1},{4,2},{5,3},{6,4},{7,5},{8,14},{9,15},{10,... | collective-permute-start | bytes 614408 | tf_op jit(solution)/shard_map/ppermute | solution.py:469
  37.9 15.0 %collective-permute-start.14 = (f32[400,128]{1,0:T(8,128)}, f32[400,128]{1,0:T(8,128)}, u32[]{:S(2)}, u32[]{:S(2)}) collective-permute-start(f32[400,128]{1,0:T(8,128)} %get-tuple-element.82), channel_id=1, source_target_pairs={{0,2},{1,3},{2,4},{3,5},{4,6},{5,7},{6,0},{7,1},{8,10},{9,11},{10,... | collective-permute-start | bytes 614408 | tf_op jit(solution)/shard_map/ppermute | solution.py:469
  39.7 13.2 %collective-permute-start.15 = (f32[400,128]{1,0:T(8,128)}, f32[400,128]{1,0:T(8,128)}, u32[]{:S(2)}, u32[]{:S(2)}) collective-permute-start(f32[400,128]{1,0:T(8,128)} %get-tuple-element.83), channel_id=1, source_target_pairs={{0,6},{1,7},{2,0},{3,1},{4,2},{5,3},{6,4},{7,5},{8,14},{9,15},{10,... | collective-permute-start | bytes 614408 | tf_op jit(solution)/shard_map/ppermute | solution.py:469
  49.1 12.1 %collective-permute-start.7 = (f32[400,128]{1,0:T(8,128)S(1)}, f32[400,128]{1,0:T(8,128)S(1)}, u32[]{:S(2)}, u32[]{:S(2)}) collective-permute-start(f32[400,128]{1,0:T(8,128)S(1)} %get-tuple-element.69), channel_id=1, source_target_pairs={{0,2},{1,3},{2,4},{3,5},{4,6},{5,7},{6,0},{7,1},{8,10},{9,11},{10,... | collective-permute-start | bytes 614408 | tf_op jit(solution)/shard_map/ppermute | solution.py:469
  50.0 12.1 %collective-permute-start.8 = (f32[400,128]{1,0:T(8,128)S(1)}, f32[400,128]{1,0:T(8,128)S(1)}, u32[]{:S(2)}, u32[]{:S(2)}) collective-permute-start(f32[400,128]{1,0:T(8,128)S(1)} %get-tuple-element.70), channel_id=1, source_target_pairs={{0,6},{1,7},{2,0},{3,1},{4,2},{5,3},{6,4},{7,5},{8,14},{9,15},{10,... | collective-permute-start | bytes 614408 | tf_op jit(solution)/shard_map/ppermute | solution.py:469
  57.3 12.1 %collective-permute-start.16 = (f32[400,128]{1,0:T(8,128)S(1)}, f32[400,128]{1,0:T(8,128)S(1)}, u32[]{:S(2)}, u32[]{:S(2)}) collective-permute-start(f32[400,128]{1,0:T(8,128)S(1)} %get-tuple-element.86), channel_id=1, source_target_pairs={{0,2},{1,3},{2,4},{3,5},{4,6},{5,7},{6,0},{7,1},{8,10},{9,11},{10,... | collective-permute-start | bytes 614408 | tf_op jit(solution)/shard_map/ppermute | solution.py:469
  57.4 12.8 %collective-permute-start.17 = (f32[400,128]{1,0:T(8,128)S(1)}, f32[400,128]{1,0:T(8,128)S(1)}, u32[]{:S(2)}, u32[]{:S(2)}) collective-permute-start(f32[400,128]{1,0:T(8,128)S(1)} %get-tuple-element.87), channel_id=1, source_target_pairs={{0,6},{1,7},{2,0},{3,1},{4,2},{5,3},{6,4},{7,5},{8,14},{9,15},{10,... | collective-permute-start | bytes 614408 | tf_op jit(solution)/shard_map/ppermute | solution.py:469
  65.5 13.5 %collective-permute-start.9 = (f32[400,128]{1,0:T(8,128)S(1)}, f32[400,128]{1,0:T(8,128)S(1)}, u32[]{:S(2)}, u32[]{:S(2)}) collective-permute-start(f32[400,128]{1,0:T(8,128)S(1)} %get-tuple-element.73), channel_id=1, source_target_pairs={{0,2},{1,3},{2,4},{3,5},{4,6},{5,7},{6,0},{7,1},{8,10},{9,11},{10,... | collective-permute-start | bytes 614408 | tf_op jit(solution)/shard_map/ppermute | solution.py:469
  66.0 13.0 %collective-permute-start.10 = (f32[400,128]{1,0:T(8,128)S(1)}, f32[400,128]{1,0:T(8,128)S(1)}, u32[]{:S(2)}, u32[]{:S(2)}) collective-permute-start(f32[400,128]{1,0:T(8,128)S(1)} %get-tuple-element.74), channel_id=1, source_target_pairs={{0,6},{1,7},{2,0},{3,1},{4,2},{5,3},{6,4},{7,5},{8,14},{9,15},{10,... | collective-permute-start | bytes 614408 | tf_op jit(solution)/shard_map/ppermute | solution.py:469
  75.2 12.7 %collective-permute-start.18 = (f32[400,128]{1,0:T(8,128)}, f32[400,128]{1,0:T(8,128)}, u32[]{:S(2)}, u32[]{:S(2)}) collective-permute-start(f32[400,128]{1,0:T(8,128)} %get-tuple-element.90), channel_id=1, source_target_pairs={{0,2},{1,3},{2,4},{3,5},{4,6},{5,7},{6,0},{7,1},{8,10},{9,11},{10,... | collective-permute-start | bytes 614408 | tf_op jit(solution)/shard_map/ppermute | solution.py:469
  75.7 12.9 %collective-permute-start.19 = (f32[400,128]{1,0:T(8,128)}, f32[400,128]{1,0:T(8,128)}, u32[]{:S(2)}, u32[]{:S(2)}) collective-permute-start(f32[400,128]{1,0:T(8,128)} %get-tuple-element.91), channel_id=1, source_target_pairs={{0,6},{1,7},{2,0},{3,1},{4,2},{5,3},{6,4},{7,5},{8,14},{9,15},{10,... | collective-permute-start | bytes 614408 | tf_op jit(solution)/shard_map/ppermute | solution.py:469
  84.0 15.3 %collective-permute-start.11 = (f32[400,128]{1,0:T(8,128)}, f32[400,128]{1,0:T(8,128)}, u32[]{:S(2)}, u32[]{:S(2)}) collective-permute-start(f32[400,128]{1,0:T(8,128)} %get-tuple-element.77), channel_id=1, source_target_pairs={{0,2},{1,3},{2,4},{3,5},{4,6},{5,7},{6,0},{7,1},{8,10},{9,11},{10,... | collective-permute-start | bytes 614408 | tf_op jit(solution)/shard_map/ppermute | solution.py:469
  84.1 15.2 %collective-permute-start.12 = (f32[400,128]{1,0:T(8,128)}, f32[400,128]{1,0:T(8,128)}, u32[]{:S(2)}, u32[]{:S(2)}) collective-permute-start(f32[400,128]{1,0:T(8,128)} %get-tuple-element.78), channel_id=1, source_target_pairs={{0,6},{1,7},{2,0},{3,1},{4,2},{5,3},{6,4},{7,5},{8,14},{9,15},{10,... | collective-permute-start | bytes 614408 | tf_op jit(solution)/shard_map/ppermute | solution.py:469
  95.4 10.9 %collective-permute-start.20 = (f32[400,128]{1,0:T(8,128)S(1)}, f32[400,128]{1,0:T(8,128)S(1)}, u32[]{:S(2)}, u32[]{:S(2)}) collective-permute-start(f32[400,128]{1,0:T(8,128)S(1)} %get-tuple-element.94), channel_id=1, source_target_pairs={{0,2},{1,3},{2,4},{3,5},{4,6},{5,7},{6,0},{7,1},{8,10},{9,11},{10,... | collective-permute-start | bytes 614408 | tf_op jit(solution)/shard_map/ppermute | solution.py:469
  95.6 10.6 %collective-permute-start.21 = (f32[400,128]{1,0:T(8,128)S(1)}, f32[400,128]{1,0:T(8,128)S(1)}, u32[]{:S(2)}, u32[]{:S(2)}) collective-permute-start(f32[400,128]{1,0:T(8,128)S(1)} %get-tuple-element.95), channel_id=1, source_target_pairs={{0,6},{1,7},{2,0},{3,1},{4,2},{5,3},{6,4},{7,5},{8,14},{9,15},{10,... | collective-permute-start | bytes 614408 | tf_op jit(solution)/shard_map/ppermute | solution.py:469
  102.7 10.6 %collective-permute-start.22 = (f32[384,128]{1,0:T(8,128)S(1)}, f32[384,128]{1,0:T(8,128)S(1)}, u32[]{:S(2)}, u32[]{:S(2)}) collective-permute-start(f32[384,128]{1,0:T(8,128)S(1)} %get-tuple-element.100), channel_id=1, source_target_pairs={{0,1},{1,0},{2,3},{3,2},{4,5},{5,4},{6,7},{7,6},{8,9},{9,8},{10,11... | collective-permute-start | bytes 589832 | tf_op jit(solution)/shard_map/ppermute | solution.py:469
  104.2 11.5 %collective-permute-start.24 = (f32[384,128]{1,0:T(8,128)S(1)}, f32[384,128]{1,0:T(8,128)S(1)}, u32[]{:S(2)}, u32[]{:S(2)}) collective-permute-start(f32[384,128]{1,0:T(8,128)S(1)} %get-tuple-element.98.refs_3_), channel_id=1, source_target_pairs={{0,16},{8,24},{16,0},{24,8},{1,17},{9,25},{17,1},{25,9},{2,18},{10... | collective-permute-start | bytes 589832 | tf_op jit(solution)/shard_map/ppermute | solution.py:469
  105.7 10.0 %collective-permute-start.25 = (f32[384,128]{1,0:T(8,128)S(1)}, f32[384,128]{1,0:T(8,128)S(1)}, u32[]{:S(2)}, u32[]{:S(2)}) collective-permute-start(f32[384,128]{1,0:T(8,128)S(1)} %get-tuple-element.102.refs_5_), channel_id=1, source_target_pairs={{0,17},{1,16},{2,19},{3,18},{4,21},{5,20},{6,23},{7,22},{8,25},{9,... | collective-permute-start | bytes 589832 | tf_op jit(solution)/shard_map/ppermute | solution.py:493
  109.0 9.8 %collective-permute-start.23 = (f32[384,128]{1,0:T(8,128)S(1)}, f32[384,128]{1,0:T(8,128)S(1)}, u32[]{:S(2)}, u32[]{:S(2)}) collective-permute-start(f32[384,128]{1,0:T(8,128)S(1)} %get-tuple-element.101), channel_id=1, source_target_pairs={{0,1},{1,0},{2,3},{3,2},{4,5},{5,4},{6,7},{7,6},{8,9},{9,8},{10,11... | collective-permute-start | bytes 589832 | tf_op jit(solution)/shard_map/ppermute | solution.py:469
  110.6 8.3 %collective-permute-start.26 = (f32[384,128]{1,0:T(8,128)S(1)}, f32[384,128]{1,0:T(8,128)S(1)}, u32[]{:S(2)}, u32[]{:S(2)}) collective-permute-start(f32[384,128]{1,0:T(8,128)S(1)} %get-tuple-element.99.refs_4_), channel_id=1, source_target_pairs={{0,16},{8,24},{16,0},{24,8},{1,17},{9,25},{17,1},{25,9},{2,18},{10... | collective-permute-start | bytes 589832 | tf_op jit(solution)/shard_map/ppermute | solution.py:469
  113.3 7.7 %collective-permute-start.27 = (f32[384,128]{1,0:T(8,128)S(1)}, f32[384,128]{1,0:T(8,128)S(1)}, u32[]{:S(2)}, u32[]{:S(2)}) collective-permute-start(f32[384,128]{1,0:T(8,128)S(1)} %get-tuple-element.103.refs_6_), channel_id=1, source_target_pairs={{0,17},{1,16},{2,19},{3,18},{4,21},{5,20},{6,23},{7,22},{8,25},{9,... | collective-permute-start | bytes 589832 | tf_op jit(solution)/shard_map/ppermute | solution.py:493
  128.3 6.6 %collective-permute-start.32 = (f32[64,512]{1,0:T(8,128)S(1)}, f32[64,512]{1,0:T(8,128)S(1)}, u32[]{:S(2)}, u32[]{:S(2)}) collective-permute-start(f32[64,512]{1,0:T(8,128)S(1)} %get-tuple-element.109), channel_id=1, source_target_pairs={{0,17},{1,16},{2,19},{3,18},{4,21},{5,20},{6,23},{7,22},{8,25},{9,... | collective-permute-start | bytes 393224 | tf_op jit(solution)/shard_map/ppermute | solution.py:493
  134.9 13.3 %collective-permute-start.33 = (f32[768,128]{1,0:T(8,128)S(1)}, f32[768,128]{1,0:T(8,128)S(1)}, u32[]{:S(2)}, u32[]{:S(2)}) collective-permute-start(f32[768,128]{1,0:T(8,128)S(1)} %get-tuple-element.110), channel_id=1, source_target_pairs={{0,1},{1,0},{2,3},{3,2},{4,5},{5,4},{6,7},{7,6},{8,9},{9,8},{10,11... | collective-permute-start | bytes 1179656 | tf_op jit(solution)/shard_map/ppermute | solution.py:469
  136.5 8.3 %collective-permute-start.34 = (f32[64,512]{1,0:T(8,128)S(1)}, f32[64,512]{1,0:T(8,128)S(1)}, u32[]{:S(2)}, u32[]{:S(2)}) collective-permute-start(f32[64,512]{1,0:T(8,128)S(1)} %shard_map.106.refs_1_), channel_id=1, source_target_pairs={{0,2},{1,3},{2,4},{3,5},{4,6},{5,7},{6,0},{7,1},{8,10},{9,11},{10,... | collective-permute-start | bytes 393224 | tf_op jit(solution)/shard_map/ppermute | solution.py:469
  136.5 11.7 %collective-permute-start.35 = (f32[64,512]{1,0:T(8,128)S(1)}, f32[64,512]{1,0:T(8,128)S(1)}, u32[]{:S(2)}, u32[]{:S(2)}) collective-permute-start(f32[64,512]{1,0:T(8,128)S(1)} %shard_map.106.refs_1_), channel_id=1, source_target_pairs={{0,4},{1,5},{2,6},{3,7},{4,0},{5,1},{6,2},{7,3},{8,12},{9,13},{10,... | collective-permute-start | bytes 393224 | tf_op jit(solution)/shard_map/ppermute | solution.py:469
  137.5 10.7 %collective-permute-start.36 = (f32[64,512]{1,0:T(8,128)S(1)}, f32[64,512]{1,0:T(8,128)S(1)}, u32[]{:S(2)}, u32[]{:S(2)}) collective-permute-start(f32[64,512]{1,0:T(8,128)S(1)} %shard_map.106.refs_1_), channel_id=1, source_target_pairs={{0,6},{1,7},{2,0},{3,1},{4,2},{5,3},{6,4},{7,5},{8,14},{9,15},{10,... | collective-permute-start | bytes 393224 | tf_op jit(solution)/shard_map/ppermute | solution.py:469
  (35 other events, 278.5 us)
